TPU v7x, 32 devices: a whole 2x2x4 slice. The times are simulated.
32 devices in a mesh: row: 8 (over y, x, core), col: 4 (over z).
Axes of the slice: x: 2, y: 2, z: 4, core: 2. Of those that a mesh axis runs over, the one named last changes fastest.
Arguments:
- image: bfloat16 [256, 512, 256], P('row', 'col'), may hold values from -60 to 60
- bn_gain: float32 [256], replicated, may hold values from 0.5 to 2
- bn_shift: float32 [256], replicated, may hold values from -3 to 3
- expand_weight: bfloat16 [256, 1024], replicated, may hold values from -0.375 to 0.375
- expand_bias: float32 [1024], replicated, may hold values from -3 to 3
- depth_kernel: bfloat16 [3, 3, 1024], replicated, may hold values from -2 to 2
- depth_bias: float32 [1024], replicated, may hold values from -3 to 3
- project_weight: bfloat16 [1024, 256], replicated, may hold values from -0.1875 to 0.1875
- norm_gain: float32 [2, 256], replicated, may hold values from 0.5 to 2
- qkv_weight: bfloat16 [2, 256, 768], replicated, may hold values from -7 to 7
- out_weight: bfloat16 [2, 256, 256], replicated, may hold values from -0.375 to 0.375
Outputs:
- features_out: bfloat16 [256, 512, 256], P('row', 'col')
All inputs are finite; a program needn't handle non-finite values.
Results may differ from a plain program's by a relative error of at most 0.011.
Values may be sent and summed in bfloat16 or wider, within the bound.
A program may use at most 128 MiB of HBM per device.

v0:
```python
import math

import jax
import jax.numpy as jnp
from jax import lax
from jax.sharding import PartitionSpec as P

HEADS = 8
WINDOW = 8
GRID_SIDE = 16


def padded(cells, sides, width):
    for axis, dim in sides:
        count = lax.axis_size(axis)
        ends = count - 1
        head = lax.slice_in_dim(cells, 0, width, axis=dim)
        tail = lax.slice_in_dim(cells, cells.shape[dim] - width, cells.shape[dim], axis=dim)
        cells = jnp.concatenate(
            [
                lax.ppermute(tail, axis, [(i, (i + 1) % count) for i in range(ends)]),
                cells,
                lax.ppermute(head, axis, [((i + 1) % count, i) for i in range(ends)]),
            ],
            axis=dim,
        )
    return cells


def layer_norm(values, gain):
    mean = jnp.mean(values, axis=-1, keepdims=True)
    centred = values - mean
    spread = jnp.mean(centred * centred, axis=-1, keepdims=True)
    return centred * lax.rsqrt(spread + 1e-05) * gain


def expand_pixels(pixels, bn_gain, bn_shift, expand_weight, expand_bias):
    shape = pixels.shape
    normed = (pixels.astype(jnp.float32) * bn_gain + bn_shift).astype(jnp.bfloat16)
    hidden = (
        jnp.dot(normed.reshape(-1, shape[-1]), expand_weight, preferred_element_type=jnp.float32)
        + expand_bias
    )
    return jax.nn.gelu(hidden).astype(jnp.bfloat16).reshape(shape[:-1] + (expand_weight.shape[1],))


def depth_project(framed, residual, depth_kernel, depth_bias, project_weight):
    height = residual.shape[0]
    width = residual.shape[1]
    kernel = depth_kernel.astype(jnp.float32)
    total = jnp.zeros((height, width, framed.shape[2]), jnp.float32)
    for down in range(3):
        for across in range(3):
            total = (
                total
                + framed[down : down + height, across : across + width].astype(jnp.float32)
                * kernel[down, across]
            )
    middle = jax.nn.gelu(total + depth_bias).astype(jnp.bfloat16)
    moved = jnp.dot(
        middle.reshape(height * width, -1), project_weight, preferred_element_type=jnp.float32
    )
    return (residual.astype(jnp.float32) + moved.reshape(height, width, -1)).astype(jnp.bfloat16)


def attend(tokens, gain, qkv_weight, out_weight):
    groups, length, chans = tokens.shape
    values = tokens.astype(jnp.float32)
    normed = layer_norm(values, gain).astype(jnp.bfloat16)
    proj = jnp.dot(
        normed.reshape(groups * length, chans), qkv_weight, preferred_element_type=jnp.float32
    ).astype(jnp.bfloat16)
    proj = proj.reshape(groups, length, 3, HEADS, chans // HEADS)
    query = proj[:, :, 0]
    keys = proj[:, :, 1]
    vals = proj[:, :, 2]
    scores = jnp.einsum("gqhd,gkhd->ghqk", query, keys, preferred_element_type=jnp.float32) * (
        chans // HEADS
    ) ** (-0.5)
    top = jnp.max(scores, axis=-1, keepdims=True)
    weights = jnp.exp(scores - top)
    probs = (weights / jnp.sum(weights, axis=-1, keepdims=True)).astype(jnp.bfloat16)
    mixed = jnp.einsum("ghqk,gkhd->gqhd", probs, vals, preferred_element_type=jnp.float32).astype(
        jnp.bfloat16
    )
    moved = jnp.dot(
        mixed.reshape(groups * length, chans), out_weight, preferred_element_type=jnp.float32
    )
    return (values + moved.reshape(groups, length, chans)).astype(jnp.bfloat16)


def attend_batched(tokens, gain, qkv_weight, out_weight, wanted):
    groups = tokens.shape[0]
    per_step = math.gcd(groups, wanted)
    stacked = tokens.reshape((groups // per_step, per_step) + tokens.shape[1:])

    def one_batch(batch):
        return attend(batch, gain, qkv_weight, out_weight)

    return lax.map(one_batch, stacked).reshape(tokens.shape)


def per_device(
    image,
    bn_gain,
    bn_shift,
    expand_weight,
    expand_bias,
    depth_kernel,
    depth_bias,
    project_weight,
    norm_gain,
    qkv_weight,
    out_weight,
):
    rows_dev, cols_dev, chans = image.shape
    row_count = lax.axis_size("row")
    col_count = lax.axis_size("col")
    strips = rows_dev // WINDOW

    def expand_strip(index):
        piece = lax.dynamic_slice_in_dim(image, index * WINDOW, WINDOW, 0)
        return expand_pixels(piece, bn_gain, bn_shift, expand_weight, expand_bias)

    hidden = lax.map(expand_strip, jnp.arange(strips)).reshape(rows_dev, cols_dev, -1)
    framed_all = padded(hidden, (("row", 0), ("col", 1)), 1)

    def mix_strip(index):
        framed = lax.dynamic_slice_in_dim(framed_all, index * WINDOW, WINDOW + 2, 0)
        residual = lax.dynamic_slice_in_dim(image, index * WINDOW, WINDOW, 0)
        return depth_project(framed, residual, depth_kernel, depth_bias, project_weight)

    after_conv = lax.map(mix_strip, jnp.arange(strips)).reshape(rows_dev, cols_dev, chans)
    windows = after_conv.reshape(
        rows_dev // WINDOW, WINDOW, cols_dev // WINDOW, WINDOW, chans
    ).transpose(0, 2, 1, 3, 4)
    windows = windows.reshape(-1, WINDOW * WINDOW, chans)
    windows = attend_batched(windows, norm_gain[0], qkv_weight[0], out_weight[0], 16)
    after_block = windows.reshape(
        rows_dev // WINDOW, cols_dev // WINDOW, WINDOW, WINDOW, chans
    ).transpose(0, 2, 1, 3, 4)
    after_block = after_block.reshape(rows_dev, cols_dev, chans)
    rep_row = GRID_SIDE // row_count
    rep_col = GRID_SIDE // col_count
    low_row = rows_dev // GRID_SIDE
    low_col = cols_dev // GRID_SIDE
    items = low_row * low_col
    local = rep_row * rep_col
    devices = row_count * col_count
    arranged = after_block.reshape(
        rep_row, row_count, low_row, rep_col, col_count, low_col, chans
    ).transpose(1, 4, 2, 5, 0, 3, 6)
    outgoing = arranged.reshape(devices, 1, items, local, chans)
    received = lax.all_to_all(outgoing, ("row", "col"), split_axis=0, concat_axis=1, tiled=True)
    count = received.shape[2]
    tokens = (
        received.reshape(devices, count, local, chans)
        .transpose(1, 0, 2, 3)
        .reshape(count, devices * local, chans)
    )
    done = attend_batched(tokens, norm_gain[1], qkv_weight[1], out_weight[1], 2)
    reply = (
        done.reshape(count, devices, local, chans)
        .transpose(1, 0, 2, 3)
        .reshape(1, devices, count, local, chans)
    )
    returned = lax.all_to_all(reply, ("row", "col"), split_axis=1, concat_axis=0, tiled=True)
    placed = returned.reshape(
        row_count, col_count, low_row, low_col, rep_row, rep_col, chans
    ).transpose(4, 0, 2, 5, 1, 3, 6)
    return placed.reshape(rows_dev, cols_dev, chans)


def solution(mesh):
    in_specs = (P("row", "col", None), P(), P(), P(), P(), P(), P(), P(), P(), P(), P())
    out_specs = P("row", "col", None)
    return jax.shard_map(
        per_device, mesh=mesh, in_specs=in_specs, out_specs=out_specs, check_vma=False
    )
```

profile of v0, /device:TPU:0, one launch (start us, length us, event | category | flops | bytes accessed | tf_op | source)
XLA Modules:
  0.0 401.2 jit_solution(823727013022699249)
XLA Ops:
  0.0 27.1 %while.40 = (s32[]{:T(128)}, bf16[4,8,128,1024]{3,2,1,0:T(8,128)(2,1)}, s32[4]{0:T(128)S(1)}, bf16[32,128,256]{2,1,0:T(8,128)(2,1)}, f32[256]{0:T(256)}, /*index...) while((s32[]{:T(128)}, ...), condition=%wide.region_1.2_spmd, body=%wide.region_0.1_spmd.sunk | while | flops 548405248 | bytes 8395443 | solution.py:125
  2.6 2.7 fusion.122
  9.3 2.7 fusion.122
  16.2 2.7 fusion.122
  23.0 2.7 fusion.122
  28.2 2.4 collective-permute-start
  33.4 2.7 collective-permute-done.1
  37.5 3.5 collective-permute-start.2
  43.6 4.4 %collective-permute-done.3 = bf16[34,1,1024]{2,1,0:T(2,128)(2,1)S(1)} collective-permute-done((bf16[34,1,1024]{2,1,0:T(2,128)(2,1)S(1)}, bf16[34,1,1024]{2,1,0:T(2,128)(2,1)S(1)}, u32[]{:S(2)}, u32[]{:S(2)}) %collective-permute-start.3) | collective-permute-done | bytes 69664 | tf_op jit(solution)/shard_map/ppermute | solution.py:23
  48.0 12.3 %pad_maximum_fusion = bf16[34,130,1024]{2,1,0:T(8,128)(2,1)} fusion(bf16[34,1,1024]{2,1,0:T(2,128)(2,1)S(1)} %collective-permute-done.3, bf16[1,128,1024]{2,1,0:T(8,128)(2,1)S(1)} %collective-permute-done.1, bf16[32,128,1024]{2,1,0:T(8,128)(2,1)} %bitcast.35, bf16[1,128,1024]{2,1,0:T(8,128)(2,1)S(1)} %collective-permute-done, ...), kind=kLoop, calls=%fused_computation.91 | loop fusion | flops 45260800 | bytes 18104320 | tf_op jit(solution)/shard_map/concatenate | solution.py:19
  60.3 63.7 %while.41 = (s32[]{:T(128)}, bf16[4,8,128,256]{3,2,1,0:T(8,128)(2,1)}, s32[4]{0:T(128)S(1)}, bf16[32,128,256]{2,1,0:T(8,128)(2,1)}, bf16[34,130,1024]{2,1,0:T(8,...) while((s32[]{:T(128)}, ...), condition=%wide.region_3.4_spmd, body=%wide.region_2.3_spmd.sunk | while | flops 575406080 | bytes 20562728 | solution.py:133
  61.6 15.1 %fusion.126 = bf16[4,8,128,256]{3,2,1,0:T(8,128)(2,1)} fusion(bf16[4,8,128,256]{3,2,1,0:T(8,128)(2,1)} %get-tuple-element.522, s32[]{:T(128)} %get-tuple-element.521, bf16[34,130,1024]{2,1,0:T(8,128)(2,1)} %get-tuple-element.540, s32[]{:T(128)S(6)} %add.362, s32[]{:T(128)S(6)} %add.363, s32[]{:T(128)S(6)} %add.364, s32[]{:T(128)S(6)} %add.365, ...), kind=kOutput, calls=%fused_computation.24.clone.1 | convolution fusion | flops 575406080 | bytes 20488728 | tf_op jit(solution)/shard_map/while/body/eval_jaxpr/dot_general | solution.py:60
  78.0 14.1 %fusion.126 = bf16[4,8,128,256]{3,2,1,0:T(8,128)(2,1)} fusion(bf16[4,8,128,256]{3,2,1,0:T(8,128)(2,1)} %get-tuple-element.522, s32[]{:T(128)} %get-tuple-element.521, bf16[34,130,1024]{2,1,0:T(8,128)(2,1)} %get-tuple-element.540, s32[]{:T(128)S(6)} %add.362, s32[]{:T(128)S(6)} %add.363, s32[]{:T(128)S(6)} %add.364, s32[]{:T(128)S(6)} %add.365, ...), kind=kOutput, calls=%fused_computation.24.clone.1 | convolution fusion | flops 575406080 | bytes 20488728 | tf_op jit(solution)/shard_map/while/body/eval_jaxpr/dot_general | solution.py:60
  93.4 14.9 %fusion.126 = bf16[4,8,128,256]{3,2,1,0:T(8,128)(2,1)} fusion(bf16[4,8,128,256]{3,2,1,0:T(8,128)(2,1)} %get-tuple-element.522, s32[]{:T(128)} %get-tuple-element.521, bf16[34,130,1024]{2,1,0:T(8,128)(2,1)} %get-tuple-element.540, s32[]{:T(128)S(6)} %add.362, s32[]{:T(128)S(6)} %add.363, s32[]{:T(128)S(6)} %add.364, s32[]{:T(128)S(6)} %add.365, ...), kind=kOutput, calls=%fused_computation.24.clone.1 | convolution fusion | flops 575406080 | bytes 20488728 | tf_op jit(solution)/shard_map/while/body/eval_jaxpr/dot_general | solution.py:60
  109.6 14.4 %fusion.126 = bf16[4,8,128,256]{3,2,1,0:T(8,128)(2,1)} fusion(bf16[4,8,128,256]{3,2,1,0:T(8,128)(2,1)} %get-tuple-element.522, s32[]{:T(128)} %get-tuple-element.521, bf16[34,130,1024]{2,1,0:T(8,128)(2,1)} %get-tuple-element.540, s32[]{:T(128)S(6)} %add.362, s32[]{:T(128)S(6)} %add.363, s32[]{:T(128)S(6)} %add.364, s32[]{:T(128)S(6)} %add.365, ...), kind=kOutput, calls=%fused_computation.24.clone.1 | convolution fusion | flops 575406080 | bytes 20488728 | tf_op jit(solution)/shard_map/while/body/eval_jaxpr/dot_general | solution.py:60
  124.0 1.9 copy_bitcast_fusion.21
  125.9 73.0 %while.42 = (s32[]{:T(128)}, bf16[4,16,64,256]{3,2,1,0:T(8,128)(2,1)}, bf16[4,16,64,256]{3,2,1,0:T(8,128)(2,1)S(1)}, f32[1,256]{1,0:T(1,128)S(1)}, bf16[256,768]...) while((s32[]{:T(128)}, bf16[4,16,64,256]{3,2,1,0:T(8,128)(2,1)}, ...), condition=%wide.region_9.10_spmd, body=%wide.region_4.9_spmd.sunk | while | flops 611845184 | bytes 43636396 | solution.py:100
  129.4 4.1 %reshape.136 = bf16[16,64,3,8,32]{1,0,4,3,2:T(8,128)(2,1)S(1)} reshape(bf16[1024,768]{0,1:T(8,128)(2,1)} %copy.132) | data formatting | bytes 3145728 | tf_op jit(solution)/shard_map/while/body/eval_jaxpr/reshape | solution.py:73
  135.1 6.2 %fusion.135 = (f32[16,8,64]{2,1,0:T(8,128)S(1)}, f32[16,8,64,64]{2,3,1,0:T(8,128)S(1)}) fusion(f32[16,8,64,64]{2,3,1,0:T(8,128)S(1)} %fusion.134), kind=kOutput, calls=%fused_computation.103.clone.1 | output fusion | flops 2097215 | bytes 4227072 | tf_op jit(solution)/shard_map/while/body/eval_jaxpr/sub | solution.py:81
  147.7 4.1 %reshape.136 = bf16[16,64,3,8,32]{1,0,4,3,2:T(8,128)(2,1)S(1)} reshape(bf16[1024,768]{0,1:T(8,128)(2,1)} %copy.132) | data formatting | bytes 3145728 | tf_op jit(solution)/shard_map/while/body/eval_jaxpr/reshape | solution.py:73
  153.3 6.2 %fusion.135 = (f32[16,8,64]{2,1,0:T(8,128)S(1)}, f32[16,8,64,64]{2,3,1,0:T(8,128)S(1)}) fusion(f32[16,8,64,64]{2,3,1,0:T(8,128)S(1)} %fusion.134), kind=kOutput, calls=%fused_computation.103.clone.1 | output fusion | flops 2097215 | bytes 4227072 | tf_op jit(solution)/shard_map/while/body/eval_jaxpr/sub | solution.py:81
  165.9 4.1 %reshape.136 = bf16[16,64,3,8,32]{1,0,4,3,2:T(8,128)(2,1)S(1)} reshape(bf16[1024,768]{0,1:T(8,128)(2,1)} %copy.132) | data formatting | bytes 3145728 | tf_op jit(solution)/shard_map/while/body/eval_jaxpr/reshape | solution.py:73
  171.6 6.2 %fusion.135 = (f32[16,8,64]{2,1,0:T(8,128)S(1)}, f32[16,8,64,64]{2,3,1,0:T(8,128)S(1)}) fusion(f32[16,8,64,64]{2,3,1,0:T(8,128)S(1)} %fusion.134), kind=kOutput, calls=%fused_computation.103.clone.1 | output fusion | flops 2097215 | bytes 4227072 | tf_op jit(solution)/shard_map/while/body/eval_jaxpr/sub | solution.py:81
  184.2 4.1 %reshape.136 = bf16[16,64,3,8,32]{1,0,4,3,2:T(8,128)(2,1)S(1)} reshape(bf16[1024,768]{0,1:T(8,128)(2,1)} %copy.132) | data formatting | bytes 3145728 | tf_op jit(solution)/shard_map/while/body/eval_jaxpr/reshape | solution.py:73
  189.8 6.2 %fusion.135 = (f32[16,8,64]{2,1,0:T(8,128)S(1)}, f32[16,8,64,64]{2,3,1,0:T(8,128)S(1)}) fusion(f32[16,8,64,64]{2,3,1,0:T(8,128)S(1)} %fusion.134), kind=kOutput, calls=%fused_computation.103.clone.1 | output fusion | flops 2097215 | bytes 4227072 | tf_op jit(solution)/shard_map/while/body/eval_jaxpr/sub | solution.py:81
  198.9 1.8 copy.68
  202.4 9.1 %all-to-all-start = ((bf16[32,1,16,8,256]{4,2,3,1,0:T(8,128)(2,1)}), bf16[32,1,16,8,256]{4,2,3,1,0:T(8,128)(2,1)S(1)}, u32[]{:S(2)}, u32[]{:S(2)}) async-start(bf16[32,1,16,8,256]{4,2,3,1,0:T(8,128)(2,1)} %bitcast.262), calls=%async_computation | async-start | bytes 4194304 | tf_op jit(solution)/shard_map/all_to_all | solution.py:154
  211.5 47.3 %all-to-all-done = bf16[32,1,16,8,256]{4,2,3,1,0:T(8,128)(2,1)S(1)} async-done(((bf16[32,1,16,8,256]{4,2,3,1,0:T(8,128)(2,1)}), bf16[32,1,16,8,256]{4,2,3,1,0:T(8,128)(2,1)S(1)}, u32[]{:S(2)}, u32[]{:S(2)}) %all-to-all-start) | async-done | bytes 2097184 | tf_op jit(solution)/shard_map/all_to_all | solution.py:154
  260.1 2.3 copy.78
  262.4 82.4 %while.43 = (s32[]{:T(128)}, bf16[8,2,256,256]{3,2,1,0:T(8,128)(2,1)}, bf16[8,2,256,256]{3,2,1,0:T(8,128)(2,1)S(1)}, f32[1,256]{1,0:T(1,128)S(1)}, bf16[256,768]...) while((s32[]{:T(128)}, bf16[8,2,256,256]{3,2,1,0:T(8,128)(2,1)}, ...), condition=%wide.region_15.16_spmd, body=%wide.region_10.15_spmd.sunk | while | flops 410256128 | bytes 34403984 | solution.py:100
  265.4 3.5 fusion.146
  268.9 2.8 fusion.147
  275.7 3.5 fusion.146
  279.2 2.8 fusion.147
  286.0 3.5 fusion.146
  289.5 2.8 fusion.147
  296.3 3.5 fusion.146
  299.8 2.8 fusion.147
  306.6 3.5 fusion.146
  310.1 2.8 fusion.147
  316.9 3.5 fusion.146
  320.4 2.8 fusion.147
  327.2 3.5 fusion.146
  330.7 2.8 fusion.147
  337.5 3.5 fusion.146
  341.0 2.8 fusion.147
  344.8 3.3 copy.118
  348.1 51.5 %all_to_all.8 = bf16[1,32,16,8,256]{4,2,3,0,1:T(8,128)(2,1)S(1)} all-to-all(bf16[1,32,16,8,256]{4,2,3,0,1:T(8,128)(2,1)S(1)} %bitcast.264), channel_id=1, replica_groups=mesh['row'=8,'col'=4] {'row','col'}, dimensions={1} | all-to-all | bytes 4194304 | tf_op jit(solution)/shard_map/all_to_all | solution.py:167
  (259 shorter events, 91.9 us)
Async XLA Ops:
  0.0 31.9 %copy-start.9 = (bf16[2,256,256]{2,1,0:T(8,128)(2,1)S(1)}, bf16[2,256,256]{2,1,0:T(8,128)(2,1)}, u32[]{:S(2)}) copy-start(bf16[2,256,256]{2,1,0:T(8,128)(2,1)} %param.29) | copy-start | bytes 786436
  0.0 32.6 %copy-start.8 = (bf16[2,256,768]{2,1,0:T(8,128)(2,1)S(1)}, bf16[2,256,768]{2,1,0:T(8,128)(2,1)}, u32[]{:S(2)}) copy-start(bf16[2,256,768]{2,1,0:T(8,128)(2,1)} %param.28) | copy-start | bytes 2359300
  28.2 5.2 %collective-permute-start = (bf16[1,128,1024]{2,1,0:T(8,128)(2,1)S(1)}, bf16[1,128,1024]{2,1,0:T(8,128)(2,1)S(1)}, u32[]{:S(2)}, u32[]{:S(2)}) collective-permute-start(bf16[1,128,1024]{2,1,0:T(8,128)(2,1)S(1)} %get-tuple-element.248), channel_id=1, source_target_pairs={{0,4},{4,8},{8,12},{12,16},{16,20},{20,24},{24,28},{1,5},{5,9},{9,... | collective-permute-start | bytes 786440 | tf_op jit(solution)/shard_map/ppermute | solution.py:21
  30.6 5.5 %collective-permute-start.1 = (bf16[1,128,1024]{2,1,0:T(8,128)(2,1)S(1)}, bf16[1,128,1024]{2,1,0:T(8,128)(2,1)S(1)}, u32[]{:S(2)}, u32[]{:S(2)}) collective-permute-start(bf16[1,128,1024]{2,1,0:T(8,128)(2,1)S(1)} %get-tuple-element.249), channel_id=1, source_target_pairs={{4,0},{8,4},{12,8},{16,12},{20,16},{24,20},{28,24},{5,1},{9,5},{13... | collective-permute-start | bytes 786440 | tf_op jit(solution)/shard_map/ppermute | solution.py:23
  33.4 9.1 %copy-start.11 = (f32[2,256]{1,0:T(2,128)S(1)}, f32[2,256]{1,0:T(2,128)}, u32[]{:S(2)}) copy-start(f32[2,256]{1,0:T(2,128)} %param.27) | copy-start | bytes 6148
  37.5 6.1 %collective-permute-start.2 = (bf16[34,1,1024]{2,1,0:T(2,128)(2,1)S(1)}, bf16[34,1,1024]{2,1,0:T(2,128)(2,1)S(1)}, u32[]{:S(2)}, u32[]{:S(2)}) collective-permute-start(bf16[34,1,1024]{2,1,0:T(2,128)(2,1)S(1)} %get-tuple-element.246), channel_id=1, source_target_pairs={{0,1},{1,2},{2,3},{4,5},{5,6},{6,7},{8,9},{9,10},{10,11},{12,13},{... | collective-permute-start | bytes 208904 | tf_op jit(solution)/shard_map/ppermute | solution.py:21
  41.0 6.9 %collective-permute-start.3 = (bf16[34,1,1024]{2,1,0:T(2,128)(2,1)S(1)}, bf16[34,1,1024]{2,1,0:T(2,128)(2,1)S(1)}, u32[]{:S(2)}, u32[]{:S(2)}) collective-permute-start(bf16[34,1,1024]{2,1,0:T(2,128)(2,1)S(1)} %get-tuple-element.247), channel_id=1, source_target_pairs={{1,0},{2,1},{3,2},{5,4},{6,5},{7,6},{9,8},{10,9},{11,10},{13,12},{... | collective-permute-start | bytes 208904 | tf_op jit(solution)/shard_map/ppermute | solution.py:23
  42.5 17.7 %copy-start.7 = (bf16[3,3,1024]{2,1,0:T(4,128)(2,1)S(1)}, bf16[3,3,1024]{2,1,0:T(4,128)(2,1)}, u32[]{:S(2)}) copy-start(bf16[3,3,1024]{2,1,0:T(4,128)(2,1)} %param.24) | copy-start | bytes 55300
  42.6 17.7 %copy-start.12 = (bf16[1024,256]{1,0:T(8,128)(2,1)S(1)}, bf16[1024,256]{1,0:T(8,128)(2,1)}, u32[]{:S(2)}) copy-start(bf16[1024,256]{1,0:T(8,128)(2,1)} %param.26) | copy-start | bytes 1572868
  42.6 17.7 %copy-start.13 = (f32[1024]{0:T(1024)S(1)}, f32[1024]{0:T(1024)}, u32[]{:S(2)}) copy-start(f32[1024]{0:T(1024)} %param.25) | copy-start | bytes 12292
  125.9 1.3 copy-start
  141.2 1.6 copy-start.1
  141.2 1.6 copy-start.6
  144.1 1.3 copy-start
  159.5 1.6 copy-start.1
  159.5 1.6 copy-start.6
  162.4 1.3 copy-start
  177.7 1.6 copy-start.1
  177.7 1.6 copy-start.6
  180.6 1.3 copy-start
  196.0 1.6 copy-start.1
  196.0 1.6 copy-start.6
  202.4 60.1 %copy-start.4 = (bf16[256,768]{1,0:T(8,128)(2,1)S(1)}, bf16[256,768]{1,0:T(8,128)(2,1)}, u32[]{:S(2)}) copy-start(bf16[256,768]{1,0:T(8,128)(2,1)} %get-tuple-element.576) | copy-start | bytes 1179652
  202.4 60.1 %copy-start.10 = (bf16[256,256]{1,0:T(8,128)(2,1)S(1)}, bf16[256,256]{1,0:T(8,128)(2,1)}, u32[]{:S(2)}) copy-start(bf16[256,256]{1,0:T(8,128)(2,1)} %get-tuple-element.577) | copy-start | bytes 393220
  202.4 56.4 %all-to-all-start = ((bf16[32,1,16,8,256]{4,2,3,1,0:T(8,128)(2,1)}), bf16[32,1,16,8,256]{4,2,3,1,0:T(8,128)(2,1)S(1)}, u32[]{:S(2)}, u32[]{:S(2)}) async-start(bf16[32,1,16,8,256]{4,2,3,1,0:T(8,128)(2,1)} %bitcast.262), calls=%async_computation | async-start | bytes 4194304 | tf_op jit(solution)/shard_map/all_to_all | solution.py:154
  258.8 1.3 copy-start.5
  262.5 1.3 copy-start.2
  268.9 2.9 copy-start.3
  272.8 1.3 copy-start.2
  279.2 2.9 copy-start.3
  283.0 1.3 copy-start.2
  289.5 2.9 copy-start.3
  293.3 1.3 copy-start.2
  299.8 2.9 copy-start.3
  303.6 1.3 copy-start.2
  310.1 2.9 copy-start.3
  313.9 1.3 copy-start.2
  320.4 2.9 copy-start.3
  324.2 1.3 copy-start.2
  330.7 2.9 copy-start.3
  334.5 1.3 copy-start.2
  341.0 2.9 copy-start.3
where the time goes:
time: 403 us; the launch traced here: 401 us
  matrix products  144 us (36%)
  local copies, waits for them, and re-layouts  74.4 us (18%)
  waiting for transfers between devices  55.4 us (14%)
  other arithmetic  51.9 us (13%)
  blocking collectives  51.5 us (13%)
  starting transfers between devices  17.8 us (4%)
  loops' own time  6.44 us (2%)
    dot_general x4, matrix products, depth_project(): jnp.dot(middle.reshape(height * width, -1), project_weight, preferred_ele...  58.5 us
    all_to_all x1, blocking collectives, per_device(): lax.all_to_all(reply, ('row', 'col'), split_axis=1, concat_axis=0, tiled=...  51.5 us
    all_to_all x1, waiting for transfers between devices, per_device(): lax.all_to_all(outgoing, ('row', 'col'), split_axis=0, concat_axis=1, til...  47.3 us
    sub x8, matrix products, attend(): weights = jnp.exp(scores - top)  27.9 us
    dot_general x12, matrix products, attend(): jnp.einsum('ghqk,gkhd->gqhd', probs, vals, preferred_element_type=jnp.flo...  24.9 us
    sub x4, other arithmetic, attend(): weights = jnp.exp(scores - top)  24.6 us
    reshape x12, local copies, waits for them, and re-layouts, attend(): proj = proj.reshape(groups, length, 3, HEADS, chans // HEADS)  17.9 us
    dot_general x12, matrix products, attend(): jnp.dot(mixed.reshape(groups * length, chans), out_weight, preferred_elem...  13 us
  transfers between devices with their start and end apart: 5, of which 4 were waited for; matrix products, arithmetic and copies ran while one was open for 0% of the time, Pallas kernels for 0%

commit v1 on v0

--- a/solution.py
+++ b/solution.py
@@ -3,6 +3,8 @@
 import jax
 import jax.numpy as jnp
 from jax import lax
+from jax.experimental import pallas as pl
+from jax.experimental.pallas import tpu as pltpu
 from jax.sharding import PartitionSpec as P
 
 HEADS = 8
@@ -171,9 +173,287 @@
     return placed.reshape(rows_dev, cols_dev, chans)
 
 
+NT = (((1,), (1,)), ((), ()))
+TN = (((0,), (0,)), ((), ()))
+F32 = jnp.float32
+BF16 = jnp.bfloat16
+GELU_IN = math.sqrt(2.0 / math.pi)
+
+
+def dot(a, b, dims=(((1,), (0,)), ((), ()))):
+    return lax.dot_general(a, b, dims, preferred_element_type=F32)
+
+
+def gelu_bf16(x):
+    x = x.astype(BF16)
+    inner = x * (x * x * BF16(GELU_IN * 0.044715) + BF16(GELU_IN))
+    half = x * BF16(0.5)
+    return half + half * jnp.tanh(inner)
+
+
+def norm_rows(x, gain):
+    mean = jnp.mean(x, axis=-1, keepdims=True)
+    centred = x - mean
+    spread = jnp.mean(centred * centred, axis=-1, keepdims=True)
+    return (centred * lax.rsqrt(spread + 1e-05) * gain).astype(BF16)
+
+
+def head_rows(q_t, head, size):
+    chans, width = q_t.shape
+    parts = []
+    if head:
+        parts.append(jnp.zeros((head * size, width), BF16))
+    parts.append(q_t[head * size : (head + 1) * size])
+    if (head + 1) * size < chans:
+        parts.append(jnp.zeros((chans - (head + 1) * size, width), BF16))
+    return jnp.concatenate(parts, axis=0)
+
+
+def project_qkv(x, gain, wq_t, wk, wv_t, size):
+    ln = norm_rows(x, gain)
+    scale = math.log2(math.e) / math.sqrt(size)
+    q_t = (dot(wq_t, ln, NT) * scale).astype(BF16)
+    k = dot(ln, wk).astype(BF16)
+    v_t = dot(wv_t, ln, NT).astype(BF16)
+    return q_t, k, v_t
+
+
+def window_attend(x, gain, wq_t, wk, wv_t, wo):
+    tokens, chans = x.shape
+    size = chans // HEADS
+    q_t, k, v_t = project_qkv(x, gain, wq_t, wk, wv_t, size)
+    lane = lax.broadcasted_iota(jnp.int32, (64, 256), 1)
+    low = (lane % 128) < 64
+    low_mask = low.astype(F32).astype(BF16)
+    high_mask = (1.0 - low.astype(F32)).astype(BF16)
+    ones = jnp.ones((16, 128), BF16)
+    columns = []
+    for pair in range(tokens // 128):
+        at = slice(pair * 128, pair * 128 + 128)
+        k_p = k[at]
+        mixed = []
+        for h in range(0, HEADS, 2):
+            rhs = jnp.concatenate(
+                [head_rows(q_t[:, at], h, size), head_rows(q_t[:, at], h + 1, size)], axis=1
+            )
+            s = dot(k_p, rhs)
+            s = jnp.where(low, s[:64], s[64:])
+            p = jnp.exp2(s - jnp.max(s, axis=0, keepdims=True)).astype(BF16)
+            p = jnp.concatenate([p * low_mask, p * high_mask], axis=0)
+            lhs = jnp.concatenate([v_t[h * size : (h + 2) * size, at], ones], axis=0)
+            o = dot(lhs, p)
+            inv = 1.0 / o[2 * size : 2 * size + 1]
+            mixed.append((o[:size, :128] * inv[:, :128]).astype(BF16))
+            mixed.append((o[size : 2 * size, 128:] * inv[:, 128:]).astype(BF16))
+        columns.append(jnp.concatenate(mixed, axis=0))
+    mixed_t = jnp.concatenate(columns, axis=1)
+    return x + dot(mixed_t, wo, TN)
+
+
+def set_attend(x, gain, wq_t, wk, wv_t, wo):
+    tokens, chans = x.shape
+    size = chans // HEADS
+    q_t, k, v_t = project_qkv(x, gain, wq_t, wk, wv_t, size)
+    ones = jnp.ones((16, tokens), BF16)
+    mixed = []
+    for h in range(HEADS):
+        s = dot(k, head_rows(q_t, h, size))
+        p = jnp.exp2(s - jnp.max(s, axis=0, keepdims=True)).astype(BF16)
+        lhs = jnp.concatenate([v_t[h * size : (h + 1) * size], ones], axis=0)
+        o = dot(lhs, p)
+        mixed.append((o[:size] * (1.0 / o[size : size + 1])).astype(BF16))
+    return x + dot(jnp.concatenate(mixed, axis=0), wo, TN)
+
+
+def put_halves(ref, rows, value):
+    ref[0, rows, :] = value[:, :128]
+    ref[1, rows, :] = value[:, 128:]
+
+
+def strided(ref, start, count, stride):
+    rows = pl.ds(start, count, stride=stride)
+    return jnp.concatenate([ref[0, rows, :], ref[1, rows, :]], axis=1)
+
+
+def hidden_row(
+    row, img, left, right, bn_gain, bn_shift, expand_w, expand_b, edge_low, edge_high, rowbuf, hid
+):
+    gain = bn_gain[...]
+    shift = bn_shift[...]
+    put_halves(rowbuf, slice(8, 136), img[row].astype(F32) * gain + shift)
+    put_halves(rowbuf, slice(7, 8), left[pl.ds(row, 1), :] * gain + shift)
+    put_halves(rowbuf, slice(136, 137), right[pl.ds(row, 1), :] * gain + shift)
+    planes = [strided(rowbuf, 7 + j, 16, 8) for j in range(10)]
+    normed = jnp.concatenate(planes, axis=0).astype(BF16)
+    for c in range(0, expand_w.shape[1], 256):
+        h = dot(normed, expand_w[:, c : c + 256]) + expand_b[:, c : c + 256]
+        h = gelu_bf16(h).reshape(10, 16, 256)
+        hid[row, :, :, c : c + 256] = h
+        hid[row, 0, :, c : c + 256] = h[0] * edge_low
+        hid[row, 9, :, c : c + 256] = h[9] * edge_high
+
+
+def mix_row(strip, r, slot, img, depth_k, depth_b, project_w, hid, mid, moved, conv):
+    row = strip * WINDOW + r
+    for c in range(0, hid.shape[3], 256):
+        at = slice(c, c + 256)
+        for j0 in range(0, 8, 4):
+            total = None
+            for u in range(3):
+                part = None
+                for v in range(3):
+                    term = hid[row + u, j0 + v : j0 + v + 4, :, at] * depth_k[u * 3 + v : u * 3 + v + 1, at][None]
+                    part = term if part is None else part + term
+                part = part.astype(F32)
+                total = part if total is None else total + part
+            total = total + depth_b[:, at][None]
+            mid[j0 * 16 : j0 * 16 + 64, at] = gelu_bf16(total).reshape(64, 256)
+    put_halves(moved, slice(0, 128), dot(mid[...], project_w[...]))
+    base = img[row + 1].astype(F32)
+    for s in range(16):
+        value = strided(moved, s, 8, 16) + base[s * 8 : s * 8 + 8]
+        conv[slot, s, pl.ds(pl.multiple_of(r * 8, 8), 8), :] = value
+
+
+def front_kernel(
+    img, left, right, masks, bn_gain, bn_shift, expand_w, expand_b, depth_k, depth_b, project_w,
+    gain, wq_t, wk, wv_t, wo, send, rowbuf, hid, mid, moved, conv, obuf,
+):
+    edge_low = masks[0]
+    edge_high = masks[1]
+
+    def hide(row, _):
+        hidden_row(
+            row, img, left, right, bn_gain, bn_shift, expand_w, expand_b, edge_low, edge_high,
+            rowbuf, hid,
+        )
+        return 0
+
+    lax.fori_loop(0, 34, hide, 0)
+    for c in range(0, hid.shape[3], 256):
+        hid[0, :, :, c : c + 256] = hid[0, :, :, c : c + 256] * masks[2][None]
+        hid[33, :, :, c : c + 256] = hid[33, :, :, c : c + 256] * masks[3][None]
+    for half in range(2):
+        for p in range(2):
+
+            def mix(r, _):
+                mix_row(p * 2 + half, r, p, img, depth_k, depth_b, project_w, hid, mid, moved, conv)
+                return 0
+
+            lax.fori_loop(0, 8, mix, 0)
+
+        def attend_chunk(m, _):
+            x = jnp.concatenate([conv[w // 4, (w % 4) * 4 + m] for w in range(8)], axis=0)
+            value = window_attend(x, gain[...], wq_t[...], wk[...], wv_t[...], wo[...])
+            put_halves(obuf, slice(0, 512), value)
+            for d in range(32):
+                block = [strided(obuf, 2 * d + e, 8, 64) for e in range(2)]
+                send[d, half * 4 + m] = jnp.concatenate(block, axis=0).astype(BF16)
+            return 0
+
+        lax.fori_loop(0, 4, attend_chunk, 0)
+
+
+def back_kernel(received, gain, wq_t, wk, wv_t, wo, reply):
+    def one(c, _):
+        blocks = received[:, c].astype(F32)
+        done = [
+            set_attend(
+                blocks[:, e * 8 : e * 8 + 8].reshape(256, 256), gain[...], wq_t[...], wk[...], wv_t[...], wo[...]
+            ).reshape(32, 8, 256)
+            for e in range(2)
+        ]
+        reply[:, c] = jnp.concatenate(done, axis=1).astype(BF16)
+        return 0
+
+    lax.fori_loop(0, received.shape[1], one, 0)
+
+
+def shift_pair(first, last, axis):
+    count = lax.axis_size(axis)
+    ends = count - 1
+    before = lax.ppermute(last, axis, [(i, i + 1) for i in range(ends)])
+    after = lax.ppermute(first, axis, [(i + 1, i) for i in range(ends)])
+    return before, after
+
+
+def halo(image):
+    top, bottom = shift_pair(image[:1], image[-1:], "row")
+    img = jnp.concatenate([top, image, bottom], axis=0)
+    left, right = shift_pair(img[:, 0], img[:, -1], "col")
+    return img, left.astype(F32), right.astype(F32)
+
+
+def edge_masks():
+    row = lax.axis_index("row")
+    col = lax.axis_index("col")
+    s = jnp.arange(16)[:, None]
+    low = jnp.where((col == 0) & (s == 0), 0.0, 1.0)
+    high = jnp.where((col == lax.axis_size("col") - 1) & (s == 15), 0.0, 1.0)
+    top = jnp.where(row == 0, 0.0, 1.0) * jnp.ones((16, 1))
+    bottom = jnp.where(row == lax.axis_size("row") - 1, 0.0, 1.0) * jnp.ones((16, 1))
+    masks = jnp.stack([low, high, top, bottom]).astype(BF16)
+    return jnp.broadcast_to(masks, (4, 16, 256))
+
+
+def split_weights(norm_gain, qkv_weight, out_weight, s):
+    chans = qkv_weight.shape[1]
+    w = qkv_weight[s]
+    return (
+        norm_gain[s][None],
+        w[:, :chans].T,
+        w[:, chans : 2 * chans],
+        w[:, 2 * chans :].T,
+        out_weight[s],
+    )
+
+
+VMEM = pl.BlockSpec(memory_space=pltpu.VMEM)
+
+
+def per_device_fast(
+    image, bn_gain, bn_shift, expand_weight, expand_bias, depth_kernel, depth_bias, project_weight,
+    norm_gain, qkv_weight, out_weight,
+):
+    wide = expand_weight.shape[1]
+    img, left, right = halo(image)
+    masks = edge_masks()
+    send = pl.pallas_call(
+        front_kernel,
+        out_shape=jax.ShapeDtypeStruct((32, 8, 16, 256), BF16),
+        in_specs=[VMEM] * 16,
+        out_specs=VMEM,
+        scratch_shapes=[
+            pltpu.VMEM((2, 144, 128), F32),
+            pltpu.VMEM((34, 10, 16, wide), BF16),
+            pltpu.VMEM((128, wide), BF16),
+            pltpu.VMEM((2, 128, 128), F32),
+            pltpu.VMEM((2, 16, 64, 256), F32),
+            pltpu.VMEM((2, 512, 128), F32),
+        ],
+        compiler_params=pltpu.CompilerParams(vmem_limit_bytes=56 * 1024 * 1024),
+    )(
+        img, left, right, masks, bn_gain[None], bn_shift[None], expand_weight, expand_bias[None],
+        depth_kernel.reshape(9, wide), depth_bias[None], project_weight,
+        *split_weights(norm_gain, qkv_weight, out_weight, 0),
+    )
+    received = lax.all_to_all(send, ("row", "col"), split_axis=0, concat_axis=0, tiled=True)
+    reply = pl.pallas_call(
+        back_kernel,
+        out_shape=jax.ShapeDtypeStruct((32, 8, 16, 256), BF16),
+        in_specs=[VMEM] * 6,
+        out_specs=VMEM,
+        compiler_params=pltpu.CompilerParams(vmem_limit_bytes=56 * 1024 * 1024),
+    )(received, *split_weights(norm_gain, qkv_weight, out_weight, 1))
+    returned = lax.all_to_all(reply, ("row", "col"), split_axis=0, concat_axis=0, tiled=True)
+    placed = returned.reshape(8, 4, 2, 4, 2, 2, 4, 256).transpose(5, 2, 0, 6, 3, 1, 4, 7)
+    return placed.reshape(image.shape)
+
+
 def solution(mesh):
     in_specs = (P("row", "col", None), P(), P(), P(), P(), P(), P(), P(), P(), P(), P())
     out_specs = P("row", "col", None)
+    fast = mesh.shape["row"] == 8 and mesh.shape["col"] == 4
     return jax.shard_map(
-        per_device, mesh=mesh, in_specs=in_specs, out_specs=out_specs, check_vma=False
-    )
+        per_device_fast if fast else per_device, mesh=mesh, in_specs=in_specs, out_specs=out_specs, check_vma=False
+    )

time: 403 us -> 252 us (0.63)
  matrix products: 144 us -> 0 us
  Pallas kernels: 0 us -> 107 us
  local copies, waits for them, and re-layouts: 74.4 us -> 21.9 us
  other arithmetic: 51.9 us -> 4.6 us
  waiting for transfers between devices: 55.4 us -> 47.9 us
  loops' own time: 6.44 us -> 0 us
    dot_general x48 -> x0, matrix products: 116 us -> none  [the longest x4 58.5 us: depth_project(): jnp.dot(middle.reshape(height * width, -1), project_weight, preferred_ele...]
    pallas_call x0 -> x2, Pallas kernels: none -> 107 us  [the longest x1 60.5 us: per_device_fast(): pl.pallas_call(front_kernel, out_shape=jax.ShapeDtypeStruct((32, 8, 16, 2...]
    sub x8 -> x0, matrix products: 27.9 us -> none  [attend(): weights = jnp.exp(scores - top)]
    sub x4 -> x0, other arithmetic: 24.6 us -> none  [attend(): weights = jnp.exp(scores - top)]
    reshape x12 -> x3, local copies, waits for them, and re-layouts: 17.9 us -> 4.84 us  [the longest x1 2.21 us: per_device_fast(): return placed.reshape(image.shape)]
    while x73 -> x0, local copies, waits for them, and re-layouts: 12.6 us -> none
    concatenate x1, other arithmetic: 12.3 us -> 3.29 us  [halo(): img = jnp.concatenate([top, image, bottom], axis=0)]
    convert_element_type x12 -> x0, local copies, waits for them, and re-layouts: 8.83 us -> none  [attend(): proj = jnp.dot(normed.reshape(groups * length, chans), qkv_weight, prefer...]
  transfers between devices with their start and end apart: 5 -> 5, of which waited for: 4 -> 3; matrix products, arithmetic and copies ran while one was open for 0% -> 3% of each run, Pallas kernels for 0% -> 0%
where the time goes in v1:
time: 252 us; the launch traced here: 251 us
  Pallas kernels  107 us (42%)
  blocking collectives  51.7 us (21%)
  waiting for transfers between devices  47.9 us (19%)
  local copies, waits for them, and re-layouts  21.9 us (9%)
  starting transfers between devices  17.5 us (7%)
  other arithmetic  4.6 us (2%)
    pallas_call x1, Pallas kernels, per_device_fast(): pl.pallas_call(front_kernel, out_shape=jax.ShapeDtypeStruct((32, 8, 16, 2...  60.5 us
    all_to_all x1, blocking collectives, per_device_fast(): lax.all_to_all(reply, ('row', 'col'), split_axis=0, concat_axis=0, tiled=...  51.7 us
    pallas_call x1, Pallas kernels, per_device_fast(): pl.pallas_call(back_kernel, out_shape=jax.ShapeDtypeStruct((32, 8, 16, 25...  46.4 us
    all_to_all x1, waiting for transfers between devices, per_device_fast(): lax.all_to_all(send, ('row', 'col'), split_axis=0, concat_axis=0, tiled=T...  45.9 us
    all_to_all x1, starting transfers between devices, per_device_fast(): lax.all_to_all(send, ('row', 'col'), split_axis=0, concat_axis=0, tiled=T...  9.04 us
    ppermute x2, starting transfers between devices, shift_pair(): before = lax.ppermute(last, axis, [(i, i + 1) for i in range(ends)])  5.85 us
    unnamed x15, local copies, waits for them, and re-layouts  5.83 us
  transfers between devices with their start and end apart: 5, of which 3 were waited for; matrix products, arithmetic and copies ran while one was open for 3% of the time, Pallas kernels for 0%

profile of v1, /device:TPU:0, one launch (start us, length us, event | category | flops | bytes accessed | tf_op | source)
XLA Modules:
  0.0 250.5 jit_solution(10708797712568376278)
XLA Ops:
  0.0 0.0 copy-start.2
  0.0 2.8 %copy.12 = bf16[32,128,256]{2,0,1:T(8,128)(2,1)S(1)} copy(bf16[32,128,256]{2,1,0:T(8,128)(2,1)} %param.11) | data formatting | bytes 4194304 | tf_op args[0]
  2.8 0.0 copy-start
  2.9 1.3 copy-done
  4.2 0.0 copy-start.3
  4.2 0.0 copy-start.5
  4.2 0.2 fusion.2
  4.4 2.4 collective-permute-start
  6.8 1.3 collective-permute-start.1
  8.1 0.1 pad.2.clone
  8.2 0.1 pad.3.clone
  8.2 0.0 copy-done.2
  8.2 0.1 fusion.3
  8.3 0.2 copy.21
  8.5 0.7 slice_bitcast_fusion.2
  9.2 0.0 copy-done.3
  9.2 0.7 slice_bitcast_fusion.4
  9.9 0.0 copy-done.5
  9.9 0.6 fusion.4
  10.5 0.0 copy-start.4
  10.5 0.0 collective-permute-done
  10.5 1.6 collective-permute-done.1
  12.1 3.3 %pad_maximum_fusion = bf16[34,128,256]{2,0,1:T(8,128)(2,1)S(1)} fusion(bf16[1,128,256]{2,0,1:T(2,128)(2,1)S(1)} %collective-permute-done.1, bf16[32,128,256]{2,0,1:T(8,128)(2,1)} %copy-done, bf16[1,128,256]{2,0,1:T(2,128)(2,1)S(1)} %collective-permute-done), kind=kLoop, calls=%fused_computation | loop fusion | flops 6684672 | bytes 4456448 | tf_op jit(solution)/shard_map/concatenate | solution.py:382
  15.4 3.5 %collective-permute-start.2 = (bf16[34,256]{1,0:T(8,128)(2,1)S(1)}, bf16[34,256]{1,0:T(8,128)(2,1)S(1)}, u32[]{:S(2)}, u32[]{:S(2)}) collective-permute-start(bf16[34,256]{1,0:T(8,128)(2,1)S(1)} %get-tuple-element.6), channel_id=1, source_target_pairs={{0,1},{1,2},{2,3},{4,5},{5,6},{6,7},{8,9},{9,10},{10,11},{12,13},{... | collective-permute-start | bytes 52232 | tf_op jit(solution)/shard_map/ppermute | solution.py:375
  18.9 1.3 collective-permute-start.3
  20.2 0.1 maximum_maximum_fusion
  20.3 0.8 copy.17.wk
  21.0 0.0 copy-done.4
  21.0 0.6 reshape.71.depth_k
  21.7 1.9 copy.16.img
  23.5 0.0 collective-permute-done.2
  23.5 0.6 convert_element_type.12.left
  24.2 0.4 collective-permute-done.3
  24.6 0.6 convert_element_type.13.right
  25.2 0.7 broadcast_in_dim.30.masks
  25.8 60.5 %shard_map.109 = bf16[32,8,16,256]{3,2,1,0:T(8,128)(2,1)} custom-call(bf16[34,128,256]{2,1,0:T(8,128)(2,1)} %copy.16.img, f32[34,256]{1,0:T(8,128)} %convert_element_type.12.left, f32[34,256]{1,0:T(8,128)} %convert_element_type.13.right, bf16[4,16,256]{2,1,0:T(8,128)(2,1)} %broadcast_in_dim.30.masks, f32[1,256]{1,0:T(1,128)} %bitcast.32, f32[1,256]{1,0:T(1,128)} %bitcast.33, ...), custom_call_target="tpu_custom_call" | custom-call | tf_op jit(solution)/shard_map/pallas_call | solution.py:421
  86.3 9.0 %all-to-all-start = ((bf16[32,8,16,256]{3,2,1,0:T(8,128)(2,1)}), bf16[32,8,16,256]{3,2,1,0:T(8,128)(2,1)S(1)}, u32[]{:S(2)}, u32[]{:S(2)}) async-start(bf16[32,8,16,256]{3,2,1,0:T(8,128)(2,1)} %shard_map.109), calls=%async_computation | async-start | bytes 4194304 | tf_op jit(solution)/shard_map/all_to_all | solution.py:440
  95.4 0.2 copy.22
  95.5 0.7 slice_bitcast_fusion
  96.3 0.8 copy.19.wk
  97.0 45.9 %all-to-all-done.received = bf16[32,8,16,256]{3,2,1,0:T(8,128)(2,1)S(1)} async-done(((bf16[32,8,16,256]{3,2,1,0:T(8,128)(2,1)}), bf16[32,8,16,256]{3,2,1,0:T(8,128)(2,1)S(1)}, u32[]{:S(2)}, u32[]{:S(2)}) %all-to-all-start) | async-done | bytes 2097184 | tf_op jit(solution)/shard_map/all_to_all | solution.py:440
  142.9 0.0 copy-start.1
  142.9 1.3 copy-done.1
  144.2 46.4 %shard_map.110 = bf16[32,8,16,256]{3,2,1,0:T(8,128)(2,1)} custom-call(bf16[32,8,16,256]{3,2,1,0:T(8,128)(2,1)} %copy-done.1, f32[1,256]{1,0:T(1,128)} %get-tuple-element.19.gain, bf16[256,256]{1,0:T(8,128)(2,1)} %get-tuple-element.13.wq_t, bf16[256,256]{1,0:T(8,128)(2,1)} %copy.19.wk, bf16[256,256]{1,0:T(8,128)(2,1)} %get-tuple-element.11.wv_t, ...), custom_call_target="tpu_custom_call" | custom-call | tf_op jit(solution)/shard_map/pallas_call | solution.py:441
  190.6 51.7 %all_to_all.10 = bf16[32,8,16,256]{3,2,1,0:T(8,128)(2,1)S(1)} all-to-all(bf16[32,8,16,256]{3,2,1,0:T(8,128)(2,1)} %shard_map.110), channel_id=1, replica_groups=mesh['row'=8,'col'=4] {'row','col'}, dimensions={0} | all-to-all | bytes 4194304 | tf_op jit(solution)/shard_map/all_to_all | solution.py:448
  242.3 2.0 reshape.72
  244.3 4.0 %copy.20 = bf16[2,2,8,4,4,4,2,256]{7,6,5,4,3,2,1,0:T(2,128)(2,1)S(1)} copy(bf16[2,2,8,4,4,4,2,256]{7,3,0,6,4,1,5,2:T(4,128)(2,1)} %bitcast.27) | data formatting | bytes 4194304 | tf_op jit(solution)/shard_map/transpose | solution.py:449
  248.3 2.2 reshape.73
  (2 shorter events, 0.0 us)
Async XLA Ops:
  0.0 8.2 %copy-start.2 = (bf16[2,256,768]{2,1,0:T(8,128)(2,1)S(1)}, bf16[2,256,768]{2,1,0:T(8,128)(2,1)}, u32[]{:S(2)}) copy-start(bf16[2,256,768]{2,1,0:T(8,128)(2,1)} %param.20) | copy-start | bytes 2359300
  2.8 1.3 copy-start
  4.2 5.0 %copy-start.3 = (bf16[2,256,256]{2,1,0:T(8,128)(2,1)S(1)}, bf16[2,256,256]{2,1,0:T(8,128)(2,1)}, u32[]{:S(2)}) copy-start(bf16[2,256,256]{2,1,0:T(8,128)(2,1)} %param.21) | copy-start | bytes 786436
  4.2 5.7 %copy-start.5 = (f32[2,256]{1,0:T(2,128)S(1)}, f32[2,256]{1,0:T(2,128)}, u32[]{:S(2)}) copy-start(f32[2,256]{1,0:T(2,128)} %param.19) | copy-start | bytes 6148
  4.4 6.1 %collective-permute-start = (bf16[1,128,256]{2,0,1:T(2,128)(2,1)S(1)}, bf16[1,128,256]{2,0,1:T(2,128)(2,1)S(1)}, u32[]{:S(2)}, u32[]{:S(2)}) collective-permute-start(bf16[1,128,256]{2,0,1:T(2,128)(2,1)S(1)} %get-tuple-element.7), channel_id=1, source_target_pairs={{0,4},{4,8},{8,12},{12,16},{16,20},{20,24},{24,28},{1,5},{5,9},{9,... | collective-permute-start | bytes 196616 | tf_op jit(solution)/shard_map/ppermute | solution.py:375
  6.8 5.3 %collective-permute-start.1 = (bf16[1,128,256]{2,0,1:T(2,128)(2,1)S(1)}, bf16[1,128,256]{2,0,1:T(2,128)(2,1)S(1)}, u32[]{:S(2)}, u32[]{:S(2)}) collective-permute-start(bf16[1,128,256]{2,0,1:T(2,128)(2,1)S(1)} %get-tuple-element.8), channel_id=1, source_target_pairs={{4,0},{8,4},{12,8},{16,12},{20,16},{24,20},{28,24},{5,1},{9,5},{13... | collective-permute-start | bytes 196616 | tf_op jit(solution)/shard_map/ppermute | solution.py:376
  10.5 10.5 %copy-start.4 = (bf16[3,3,1024]{2,1,0:T(4,128)(2,1)S(1)}, bf16[3,3,1024]{2,1,0:T(4,128)(2,1)}, u32[]{:S(2)}) copy-start(bf16[3,3,1024]{2,1,0:T(4,128)(2,1)} %param.16) | copy-start | bytes 55300
  15.4 8.1 %collective-permute-start.2 = (bf16[34,256]{1,0:T(8,128)(2,1)S(1)}, bf16[34,256]{1,0:T(8,128)(2,1)S(1)}, u32[]{:S(2)}, u32[]{:S(2)}) collective-permute-start(bf16[34,256]{1,0:T(8,128)(2,1)S(1)} %get-tuple-element.6), channel_id=1, source_target_pairs={{0,1},{1,2},{2,3},{4,5},{5,6},{6,7},{8,9},{9,10},{10,11},{12,13},{... | collective-permute-start | bytes 52232 | tf_op jit(solution)/shard_map/ppermute | solution.py:375
  18.9 5.7 %collective-permute-start.3 = (bf16[34,256]{1,0:T(8,128)(2,1)S(1)}, bf16[34,256]{1,0:T(8,128)(2,1)S(1)}, u32[]{:S(2)}, u32[]{:S(2)}) collective-permute-start(bf16[34,256]{1,0:T(8,128)(2,1)S(1)} %get-tuple-element.5), channel_id=1, source_target_pairs={{1,0},{2,1},{3,2},{5,4},{6,5},{7,6},{9,8},{10,9},{11,10},{13,12},{... | collective-permute-start | bytes 52232 | tf_op jit(solution)/shard_map/ppermute | solution.py:376
  86.3 56.6 %all-to-all-start = ((bf16[32,8,16,256]{3,2,1,0:T(8,128)(2,1)}), bf16[32,8,16,256]{3,2,1,0:T(8,128)(2,1)S(1)}, u32[]{:S(2)}, u32[]{:S(2)}) async-start(bf16[32,8,16,256]{3,2,1,0:T(8,128)(2,1)} %shard_map.109), calls=%async_computation | async-start | bytes 4194304 | tf_op jit(solution)/shard_map/all_to_all | solution.py:440
  142.9 1.3 copy-start.1

commit v2 on v1

--- a/solution.py
+++ b/solution.py
@@ -315,17 +315,57 @@
         conv[slot, s, pl.ds(pl.multiple_of(r * 8, 8), 8), :] = value
 
 
-def front_kernel(
+def whole_wait(buf, chunk, sem):
+    part = buf.at[chunk, pl.ds(0, PEERS)]
+    pltpu.make_async_copy(part, part, sem.at[chunk]).wait()
+
+
+def block_kernel(
     img, left, right, masks, bn_gain, bn_shift, expand_w, expand_b, depth_k, depth_b, project_w,
-    gain, wq_t, wk, wv_t, wo, send, rowbuf, hid, mid, moved, conv, obuf,
+    gain0, wq0, wk0, wv0, wo0, gain1, wq1, wk1, wv1, wo1, out,
+    rowbuf, hid, mid, moved, conv, obuf, placed, send, recv, reply, back,
+    send_sem, recv_sem, reply_sem, back_sem,
 ):
+    cols = lax.axis_size("col")
+    me = lax.axis_index("row") * cols + lax.axis_index("col")
+    barrier = pltpu.get_barrier_semaphore()
+
+    def peer_of(o):
+        return lax.rem(me + o, PEERS + 1)
+
+    def place_of(peer):
+        return (lax.div(peer, cols), lax.rem(peer, cols))
+
+    def greet(o, _):
+        pl.semaphore_signal(
+            barrier, inc=1, device_id=place_of(peer_of(o)), device_id_type=pl.DeviceIdType.MESH
+        )
+        return 0
+
+    lax.fori_loop(1, PEERS + 1, greet, 0)
+
+    def scatter(chunk, src, dst, src_sem, dst_sem):
+        def push(o, _):
+            peer = peer_of(o)
+            pltpu.make_async_remote_copy(
+                src_ref=src.at[chunk, peer],
+                dst_ref=dst.at[chunk, me],
+                send_sem=src_sem.at[chunk],
+                recv_sem=dst_sem.at[chunk],
+                device_id=place_of(peer),
+                device_id_type=pl.DeviceIdType.MESH,
+            ).start()
+            return 0
+
+        lax.fori_loop(1, PEERS + 1, push, 0)
+        dst[chunk, me] = src[chunk, me]
+
     edge_low = masks[0]
     edge_high = masks[1]
 
     def hide(row, _):
         hidden_row(
-            row, img, left, right, bn_gain, bn_shift, expand_w, expand_b, edge_low, edge_high,
-            rowbuf, hid,
+            row, img, left, right, bn_gain, bn_shift, expand_w, expand_b, edge_low, edge_high, rowbuf, hid
         )
         return 0
 
@@ -333,40 +373,75 @@
     for c in range(0, hid.shape[3], 256):
         hid[0, :, :, c : c + 256] = hid[0, :, :, c : c + 256] * masks[2][None]
         hid[33, :, :, c : c + 256] = hid[33, :, :, c : c + 256] * masks[3][None]
-    for half in range(2):
-        for p in range(2):
-
-            def mix(r, _):
-                mix_row(p * 2 + half, r, p, img, depth_k, depth_b, project_w, hid, mid, moved, conv)
-                return 0
-
-            lax.fori_loop(0, 8, mix, 0)
+
+    pl.semaphore_wait(barrier, PEERS)
+
+    def one_half(half, _):
+        def mix(i, _):
+            p = lax.div(i, 8)
+            mix_row(
+                p * 2 + half, lax.rem(i, 8), p, img, depth_k, depth_b, project_w, hid, mid, moved, conv
+            )
+            return 0
+
+        lax.fori_loop(0, 16, mix, 0)
 
         def attend_chunk(m, _):
+            chunk = half * 4 + m
             x = jnp.concatenate([conv[w // 4, (w % 4) * 4 + m] for w in range(8)], axis=0)
-            value = window_attend(x, gain[...], wq_t[...], wk[...], wv_t[...], wo[...])
+            value = window_attend(x, gain0[...], wq0[...], wk0[...], wv0[...], wo0[...])
             put_halves(obuf, slice(0, 512), value)
-            for d in range(32):
+            for d in range(PEERS + 1):
                 block = [strided(obuf, 2 * d + e, 8, 64) for e in range(2)]
-                send[d, half * 4 + m] = jnp.concatenate(block, axis=0).astype(BF16)
+                send[chunk, d] = jnp.concatenate(block, axis=0).astype(BF16)
+            scatter(chunk, send, recv, send_sem, recv_sem)
             return 0
 
         lax.fori_loop(0, 4, attend_chunk, 0)
-
-
-def back_kernel(received, gain, wq_t, wk, wv_t, wo, reply):
-    def one(c, _):
-        blocks = received[:, c].astype(F32)
+        return 0
+
+    lax.fori_loop(0, 2, one_half, 0)
+
+    def grid_chunk(chunk, _):
+        whole_wait(recv, chunk, recv_sem)
+        blocks = recv[chunk].astype(F32)
         done = [
             set_attend(
-                blocks[:, e * 8 : e * 8 + 8].reshape(256, 256), gain[...], wq_t[...], wk[...], wv_t[...], wo[...]
+                blocks[:, e * 8 : e * 8 + 8].reshape(256, 256), gain1[...], wq1[...], wk1[...], wv1[...], wo1[...]
             ).reshape(32, 8, 256)
             for e in range(2)
         ]
-        reply[:, c] = jnp.concatenate(done, axis=1).astype(BF16)
-        return 0
-
-    lax.fori_loop(0, received.shape[1], one, 0)
+        reply[chunk] = jnp.concatenate(done, axis=1).astype(BF16)
+        scatter(chunk, reply, back, reply_sem, back_sem)
+        return 0
+
+    lax.fori_loop(0, CHUNKS, grid_chunk, 0)
+
+    def finish(chunk, _):
+        whole_wait(back, chunk, back_sem)
+        half = lax.div(chunk, 4)
+        m = lax.rem(chunk, 4)
+        put_halves(obuf, slice(0, 512), back[chunk].astype(F32).reshape(512, 256))
+        for w in range(8):
+            value = strided(obuf, w, 64, 8).reshape(8, 8, 256)
+            rows = pl.ds((w // 4) * 16 + half * 8, 8)
+            placed[rows, pl.ds(pl.multiple_of((w % 4) * 32 + m * 8, 8), 8), :] = value
+        return 0
+
+    lax.fori_loop(0, CHUNKS, finish, 0)
+
+    def store(row, _):
+        out[row] = placed[row].astype(BF16)
+        return 0
+
+    lax.fori_loop(0, 32, store, 0)
+
+    def drain(chunk, _):
+        whole_wait(send, chunk, send_sem)
+        whole_wait(reply, chunk, reply_sem)
+        return 0
+
+    lax.fori_loop(0, CHUNKS, drain, 0)
 
 
 def shift_pair(first, last, axis):
@@ -408,6 +483,8 @@
     )
 
 
+PEERS = 31
+CHUNKS = 8
 VMEM = pl.BlockSpec(memory_space=pltpu.VMEM)
 
 
@@ -418,10 +495,12 @@
     wide = expand_weight.shape[1]
     img, left, right = halo(image)
     masks = edge_masks()
-    send = pl.pallas_call(
-        front_kernel,
-        out_shape=jax.ShapeDtypeStruct((32, 8, 16, 256), BF16),
-        in_specs=[VMEM] * 16,
+    blocks = pltpu.VMEM((CHUNKS, PEERS + 1, 16, 256), BF16)
+    sems = pltpu.SemaphoreType.DMA((CHUNKS,))
+    return pl.pallas_call(
+        block_kernel,
+        out_shape=jax.ShapeDtypeStruct(image.shape, BF16),
+        in_specs=[VMEM] * 21,
         out_specs=VMEM,
         scratch_shapes=[
             pltpu.VMEM((2, 144, 128), F32),
@@ -430,24 +509,19 @@
             pltpu.VMEM((2, 128, 128), F32),
             pltpu.VMEM((2, 16, 64, 256), F32),
             pltpu.VMEM((2, 512, 128), F32),
+            pltpu.VMEM(image.shape, F32),
+            blocks, blocks, blocks, blocks,
+            sems, sems, sems, sems,
         ],
-        compiler_params=pltpu.CompilerParams(vmem_limit_bytes=56 * 1024 * 1024),
+        compiler_params=pltpu.CompilerParams(
+            collective_id=0, has_side_effects=True, vmem_limit_bytes=56 * 1024 * 1024
+        ),
     )(
         img, left, right, masks, bn_gain[None], bn_shift[None], expand_weight, expand_bias[None],
         depth_kernel.reshape(9, wide), depth_bias[None], project_weight,
         *split_weights(norm_gain, qkv_weight, out_weight, 0),
-    )
-    received = lax.all_to_all(send, ("row", "col"), split_axis=0, concat_axis=0, tiled=True)
-    reply = pl.pallas_call(
-        back_kernel,
-        out_shape=jax.ShapeDtypeStruct((32, 8, 16, 256), BF16),
-        in_specs=[VMEM] * 6,
-        out_specs=VMEM,
-        compiler_params=pltpu.CompilerParams(vmem_limit_bytes=56 * 1024 * 1024),
-    )(received, *split_weights(norm_gain, qkv_weight, out_weight, 1))
-    returned = lax.all_to_all(reply, ("row", "col"), split_axis=0, concat_axis=0, tiled=True)
-    placed = returned.reshape(8, 4, 2, 4, 2, 2, 4, 256).transpose(5, 2, 0, 6, 3, 1, 4, 7)
-    return placed.reshape(image.shape)
+        *split_weights(norm_gain, qkv_weight, out_weight, 1),
+    )
 
 
 def solution(mesh):

time: 252 us -> 157 us (0.62)
  blocking collectives: 51.7 us -> 0 us
  waiting for transfers between devices: 47.9 us -> 0.01 us
  Pallas kernels: 107 us -> 126 us
  local copies, waits for them, and re-layouts: 21.9 us -> 14.9 us
  starting transfers between devices: 17.5 us -> 10.6 us
    all_to_all x1 -> x0, blocking collectives: 51.7 us -> none  [per_device_fast(): lax.all_to_all(reply, ('row', 'col'), split_axis=0, concat_axis=0, tiled=...]
    all_to_all x1 -> x0, waiting for transfers between devices: 45.9 us -> none  [per_device_fast(): lax.all_to_all(send, ('row', 'col'), split_axis=0, concat_axis=0, tiled=T...]
    pallas_call x2 -> x1, Pallas kernels: 107 us -> 126 us  [per_device_fast(): pl.pallas_call(block_kernel, out_shape=jax.ShapeDtypeStruct(image.shape,...]
    all_to_all x1 -> x0, starting transfers between devices: 9.04 us -> none  [per_device_fast(): lax.all_to_all(send, ('row', 'col'), split_axis=0, concat_axis=0, tiled=T...]
    reshape x2 -> x0, local copies, waits for them, and re-layouts: 4.22 us -> none  [the longest x1 2.21 us: per_device_fast(): return placed.reshape(image.shape)]
    transpose x1 -> x0, local copies, waits for them, and re-layouts: 4.03 us -> none  [per_device_fast(): returned.reshape(8, 4, 2, 4, 2, 2, 4, 256).transpose(5, 2, 0, 6, 3, 1, 4, 7)]
    unnamed x15 -> x14, local copies, waits for them, and re-layouts: 5.83 us -> 7.64 us
  transfers between devices with their start and end apart: 5 -> 4, of which waited for: 3 -> 0; matrix products, arithmetic and copies ran while one was open for 3% -> 5% of each run, Pallas kernels for 0% -> 0%
where the time goes in v2:
time: 157 us; the launch traced here: 156 us
  Pallas kernels  126 us (80%)
  local copies, waits for them, and re-layouts  14.9 us (9%)
  starting transfers between devices  10.6 us (7%)
  other arithmetic  4.62 us (3%)
    pallas_call x1, Pallas kernels, per_device_fast(): pl.pallas_call(block_kernel, out_shape=jax.ShapeDtypeStruct(image.shape,...  126 us
    ppermute x2, starting transfers between devices, shift_pair(): before = lax.ppermute(last, axis, [(i, i + 1) for i in range(ends)])  7.97 us
    unnamed x14, local copies, waits for them, and re-layouts  7.64 us
    concatenate x1, other arithmetic, halo(): img = jnp.concatenate([top, image, bottom], axis=0)  3.3 us
  transfers between devices with their start and end apart: 4, of which 0 were waited for; matrix products, arithmetic and copies ran while one was open for 5% of the time, Pallas kernels for 0%

profile of v2, /device:TPU:0, one launch (start us, length us, event | category | flops | bytes accessed | tf_op | source)
XLA Modules:
  0.0 156.4 jit_solution(3756128473384855655)
XLA Ops:
  0.0 0.0 copy-start.4
  0.0 0.0 copy-start.1
  0.0 2.8 %copy.12 = bf16[32,128,256]{2,0,1:T(8,128)(2,1)S(1)} copy(bf16[32,128,256]{2,1,0:T(8,128)(2,1)} %param.11) | data formatting | bytes 4194304 | tf_op args[0]
  2.8 0.0 copy-start
  2.9 1.3 copy-done
  4.2 0.0 copy-start.2
  4.2 0.2 fusion.2
  4.4 1.3 collective-permute-start.1
  5.7 3.0 %collective-permute-start = (bf16[1,128,256]{2,0,1:T(2,128)(2,1)S(1)}, bf16[1,128,256]{2,0,1:T(2,128)(2,1)S(1)}, u32[]{:S(2)}, u32[]{:S(2)}) collective-permute-start(bf16[1,128,256]{2,0,1:T(2,128)(2,1)S(1)} %get-tuple-element.7), channel_id=1, source_target_pairs={{0,4},{4,8},{8,12},{12,16},{16,20},{20,24},{24,28},{1,5},{5,9},{9,... | collective-permute-start | bytes 196616 | tf_op jit(solution)/shard_map/ppermute | solution.py:450
  8.8 0.1 pad.3.clone
  8.8 0.1 pad.2.clone
  8.9 0.0 copy-done.4
  8.9 0.6 fusion.4
  9.5 0.0 copy-done.1
  9.5 0.1 fusion.3
  9.6 0.2 copy.21
  9.7 0.2 copy.20
  9.9 0.0 copy-done.2
  9.9 0.7 slice_bitcast_fusion.4
  10.6 0.8 slice_bitcast_fusion
  11.5 0.0 copy-start.3
  11.5 0.0 collective-permute-done.1
  11.5 0.0 collective-permute-done
  11.5 3.3 %pad_maximum_fusion = bf16[34,128,256]{2,0,1:T(8,128)(2,1)S(1)} fusion(bf16[1,128,256]{2,0,1:T(2,128)(2,1)S(1)} %collective-permute-done.1, bf16[32,128,256]{2,0,1:T(8,128)(2,1)} %copy-done, bf16[1,128,256]{2,0,1:T(2,128)(2,1)S(1)} %collective-permute-done), kind=kLoop, calls=%fused_computation | loop fusion | flops 6684672 | bytes 4456448 | tf_op jit(solution)/shard_map/concatenate | solution.py:457
  14.8 4.9 %collective-permute-start.2 = (bf16[34,256]{1,0:T(8,128)(2,1)S(1)}, bf16[34,256]{1,0:T(8,128)(2,1)S(1)}, u32[]{:S(2)}, u32[]{:S(2)}) collective-permute-start(bf16[34,256]{1,0:T(8,128)(2,1)S(1)} %get-tuple-element.6), channel_id=1, source_target_pairs={{0,1},{1,2},{2,3},{4,5},{5,6},{6,7},{8,9},{9,10},{10,11},{12,13},{... | collective-permute-start | bytes 52232 | tf_op jit(solution)/shard_map/ppermute | solution.py:450
  19.7 1.3 collective-permute-start.3
  21.0 0.1 maximum_maximum_fusion
  21.1 0.0 copy-done.3
  21.1 0.6 reshape.65.depth_k
  21.7 0.8 copy.18.wk0
  22.5 0.8 copy.19.wk1
  23.3 1.9 %copy.17.img = bf16[34,128,256]{2,1,0:T(8,128)(2,1)} copy(bf16[34,128,256]{2,0,1:T(8,128)(2,1)S(1)} %pad_maximum_fusion) | data formatting | bytes 4456448 | tf_op jit(solution)/shard_map/concatenate | solution.py:457
  25.1 0.0 collective-permute-done.2
  25.1 0.6 convert_element_type.12.left
  25.7 0.0 collective-permute-done.3
  25.7 0.6 convert_element_type.13.right
  26.4 0.7 broadcast_in_dim.30.masks
  27.1 126.2 %shard_map.109 = bf16[32,128,256]{2,1,0:T(8,128)(2,1)} custom-call(bf16[34,128,256]{2,1,0:T(8,128)(2,1)} %copy.17.img, f32[34,256]{1,0:T(8,128)} %convert_element_type.12.left, f32[34,256]{1,0:T(8,128)} %convert_element_type.13.right, bf16[4,16,256]{2,1,0:T(8,128)(2,1)} %broadcast_in_dim.30.masks, f32[1,256]{1,0:T(1,128)} %bitcast.28, f32[1,256]{1,0:T(1,128)} %bitcast.29, ...), custom_call_target="tpu_custom_call" | custom-call | tf_op jit(solution)/shard_map/pallas_call | solution.py:500
  153.3 3.1 %copy.23 = bf16[32,128,256]{2,1,0:T(8,128)(2,1)} copy(bf16[32,128,256]{2,1,0:T(8,128)(2,1)} %shard_map.109) | data formatting | bytes 4194304
  (2 shorter events, 0.0 us)
Async XLA Ops:
  0.0 8.9 %copy-start.4 = (f32[2,256]{1,0:T(2,128)S(1)}, f32[2,256]{1,0:T(2,128)}, u32[]{:S(2)}) copy-start(f32[2,256]{1,0:T(2,128)} %param.19) | copy-start | bytes 6148
  0.0 9.5 %copy-start.1 = (bf16[2,256,768]{2,1,0:T(8,128)(2,1)S(1)}, bf16[2,256,768]{2,1,0:T(8,128)(2,1)}, u32[]{:S(2)}) copy-start(bf16[2,256,768]{2,1,0:T(8,128)(2,1)} %param.20) | copy-start | bytes 2359300
  2.8 1.3 copy-start
  4.2 5.7 %copy-start.2 = (bf16[2,256,256]{2,1,0:T(8,128)(2,1)S(1)}, bf16[2,256,256]{2,1,0:T(8,128)(2,1)}, u32[]{:S(2)}) copy-start(bf16[2,256,256]{2,1,0:T(8,128)(2,1)} %param.21) | copy-start | bytes 786436
  4.4 7.1 %collective-permute-start.1 = (bf16[1,128,256]{2,0,1:T(2,128)(2,1)S(1)}, bf16[1,128,256]{2,0,1:T(2,128)(2,1)S(1)}, u32[]{:S(2)}, u32[]{:S(2)}) collective-permute-start(bf16[1,128,256]{2,0,1:T(2,128)(2,1)S(1)} %get-tuple-element.8), channel_id=1, source_target_pairs={{4,0},{8,4},{12,8},{16,12},{20,16},{24,20},{28,24},{5,1},{9,5},{13... | collective-permute-start | bytes 196616 | tf_op jit(solution)/shard_map/ppermute | solution.py:451
  5.7 5.8 %collective-permute-start = (bf16[1,128,256]{2,0,1:T(2,128)(2,1)S(1)}, bf16[1,128,256]{2,0,1:T(2,128)(2,1)S(1)}, u32[]{:S(2)}, u32[]{:S(2)}) collective-permute-start(bf16[1,128,256]{2,0,1:T(2,128)(2,1)S(1)} %get-tuple-element.7), channel_id=1, source_target_pairs={{0,4},{4,8},{8,12},{12,16},{16,20},{20,24},{24,28},{1,5},{5,9},{9,... | collective-permute-start | bytes 196616 | tf_op jit(solution)/shard_map/ppermute | solution.py:450
  11.5 9.7 %copy-start.3 = (bf16[3,3,1024]{2,1,0:T(4,128)(2,1)S(1)}, bf16[3,3,1024]{2,1,0:T(4,128)(2,1)}, u32[]{:S(2)}) copy-start(bf16[3,3,1024]{2,1,0:T(4,128)(2,1)} %param.16) | copy-start | bytes 55300
  14.8 10.3 %collective-permute-start.2 = (bf16[34,256]{1,0:T(8,128)(2,1)S(1)}, bf16[34,256]{1,0:T(8,128)(2,1)S(1)}, u32[]{:S(2)}, u32[]{:S(2)}) collective-permute-start(bf16[34,256]{1,0:T(8,128)(2,1)S(1)} %get-tuple-element.6), channel_id=1, source_target_pairs={{0,1},{1,2},{2,3},{4,5},{5,6},{6,7},{8,9},{9,10},{10,11},{12,13},{... | collective-permute-start | bytes 52232 | tf_op jit(solution)/shard_map/ppermute | solution.py:450
  19.7 6.0 %collective-permute-start.3 = (bf16[34,256]{1,0:T(8,128)(2,1)S(1)}, bf16[34,256]{1,0:T(8,128)(2,1)S(1)}, u32[]{:S(2)}, u32[]{:S(2)}) collective-permute-start(bf16[34,256]{1,0:T(8,128)(2,1)S(1)} %get-tuple-element.5), channel_id=1, source_target_pairs={{1,0},{2,1},{3,2},{5,4},{6,5},{7,6},{9,8},{10,9},{11,10},{13,12},{... | collective-permute-start | bytes 52232 | tf_op jit(solution)/shard_map/ppermute | solution.py:451

commit v3 on v2

--- a/solution.py
+++ b/solution.py
@@ -276,11 +276,11 @@
 
 
 def hidden_row(
-    row, img, left, right, bn_gain, bn_shift, expand_w, expand_b, edge_low, edge_high, rowbuf, hid
+    row, cells, left, right, bn_gain, bn_shift, expand_w, expand_b, edge_low, edge_high, rowbuf, hid
 ):
     gain = bn_gain[...]
     shift = bn_shift[...]
-    put_halves(rowbuf, slice(8, 136), img[row].astype(F32) * gain + shift)
+    put_halves(rowbuf, slice(8, 136), cells.astype(F32) * gain + shift)
     put_halves(rowbuf, slice(7, 8), left[pl.ds(row, 1), :] * gain + shift)
     put_halves(rowbuf, slice(136, 137), right[pl.ds(row, 1), :] * gain + shift)
     planes = [strided(rowbuf, 7 + j, 16, 8) for j in range(10)]
@@ -288,8 +288,8 @@
     for c in range(0, expand_w.shape[1], 256):
         h = dot(normed, expand_w[:, c : c + 256]) + expand_b[:, c : c + 256]
         h = gelu_bf16(h).reshape(10, 16, 256)
-        hid[row, :, :, c : c + 256] = h
         hid[row, 0, :, c : c + 256] = h[0] * edge_low
+        hid[row, 1:9, :, c : c + 256] = h[1:9]
         hid[row, 9, :, c : c + 256] = h[9] * edge_high
 
 
@@ -302,14 +302,14 @@
             for u in range(3):
                 part = None
                 for v in range(3):
-                    term = hid[row + u, j0 + v : j0 + v + 4, :, at] * depth_k[u * 3 + v : u * 3 + v + 1, at][None]
+                    term = hid[row + u, j0 + v : j0 + v + 4, :, at] * depth_k[u, v : v + 1, at][None]
                     part = term if part is None else part + term
                 part = part.astype(F32)
                 total = part if total is None else total + part
             total = total + depth_b[:, at][None]
             mid[j0 * 16 : j0 * 16 + 64, at] = gelu_bf16(total).reshape(64, 256)
     put_halves(moved, slice(0, 128), dot(mid[...], project_w[...]))
-    base = img[row + 1].astype(F32)
+    base = img[row].astype(F32)
     for s in range(16):
         value = strided(moved, s, 8, 16) + base[s * 8 : s * 8 + 8]
         conv[slot, s, pl.ds(pl.multiple_of(r * 8, 8), 8), :] = value
@@ -321,10 +321,10 @@
 
 
 def block_kernel(
-    img, left, right, masks, bn_gain, bn_shift, expand_w, expand_b, depth_k, depth_b, project_w,
-    gain0, wq0, wk0, wv0, wo0, gain1, wq1, wk1, wv1, wo1, out,
-    rowbuf, hid, mid, moved, conv, obuf, placed, send, recv, reply, back,
-    send_sem, recv_sem, reply_sem, back_sem,
+    img, bn_gain, bn_shift, expand_w, expand_b, depth_k, depth_b, project_w,
+    norm_gain, qkv_w, out_w, out,
+    rowbuf, hid, mid, moved, conv, obuf, placed, rows_in, ends_out, ends_in, turned,
+    send, recv, reply, back, halo_sem, send_sem, recv_sem, reply_sem, back_sem,
 ):
     cols = lax.axis_size("col")
     me = lax.axis_index("row") * cols + lax.axis_index("col")
@@ -360,36 +360,102 @@
         lax.fori_loop(1, PEERS + 1, push, 0)
         dst[chunk, me] = src[chunk, me]
 
-    edge_low = masks[0]
-    edge_high = masks[1]
-
-    def hide(row, _):
+    my_row = lax.axis_index("row")
+    my_col = lax.axis_index("col")
+    row_count = lax.axis_size("row")
+    pl.semaphore_wait(barrier, PEERS)
+
+    def ring_copy(src, dst, sem, place):
+        return pltpu.make_async_remote_copy(
+            src_ref=src,
+            dst_ref=dst,
+            send_sem=halo_sem.at[sem],
+            recv_sem=halo_sem.at[sem + 1],
+            device_id=place,
+            device_id_type=pl.DeviceIdType.MESH,
+        )
+
+    below = lax.rem(my_row + 1, row_count)
+    above = lax.rem(my_row + row_count - 1, row_count)
+    after = lax.rem(my_col + 1, cols)
+    before = lax.rem(my_col + cols - 1, cols)
+    down = ring_copy(img.at[31], rows_in.at[0], 0, (below, my_col))
+    up = ring_copy(img.at[0], rows_in.at[1], 2, (above, my_col))
+    down.start()
+    up.start()
+    chans = img.shape[2]
+    for n in range(2):
+        ends_out[n, 32:40, :] = jnp.zeros((8, chans), F32)
+    for s in range(2):
+        for n in range(2):
+            part = qkv_w[s, :, n * 2 * chans : (n * 2 + 1) * chans]
+            turned[s, n] = part.astype(F32).T.astype(BF16)
+    for row in range(32):
+        cells = img[row].astype(F32)
+        ends_out[0, row + 1 : row + 2, :] = cells[:1]
+        ends_out[1, row + 1 : row + 2, :] = cells[127:]
+    down.wait()
+    up.wait()
+    for n, row in ((0, 0), (1, 33)):
+        cells = rows_in[n].astype(F32)
+        ends_out[0, row : row + 1, :] = cells[:1]
+        ends_out[1, row : row + 1, :] = cells[127:]
+    forth = ring_copy(ends_out.at[1], ends_in.at[0], 4, (my_row, after))
+    aft = ring_copy(ends_out.at[0], ends_in.at[1], 6, (my_row, before))
+    forth.start()
+    aft.start()
+    spot = lax.broadcasted_iota(jnp.int32, (16, chans), 0)
+    edge_low = jnp.where((spot == 0) & (my_col == 0), 0.0, 1.0).astype(BF16)
+    edge_high = jnp.where((spot == 15) & (my_col == cols - 1), 0.0, 1.0).astype(BF16)
+    every = jnp.ones((16, chans), F32)
+    edge_top = jnp.where(my_row == 0, 0.0, every).astype(BF16)
+    edge_bottom = jnp.where(my_row == row_count - 1, 0.0, every).astype(BF16)
+    forth.wait()
+    aft.wait()
+
+    def hide_row(row, cells, slot):
         hidden_row(
-            row, img, left, right, bn_gain, bn_shift, expand_w, expand_b, edge_low, edge_high, rowbuf, hid
+            row, cells, ends_in.at[0], ends_in.at[1], bn_gain, bn_shift, expand_w, expand_b, edge_low, edge_high,
+            rowbuf.at[slot], hid,
         )
-        return 0
-
-    lax.fori_loop(0, 34, hide, 0)
+
+    def hide(i, _):
+        for k in range(2):
+            hide_row(2 * i + k + 1, img[2 * i + k], k)
+        return 0
+
+    lax.fori_loop(0, 16, hide, 0)
+    hide_row(0, rows_in[0], 0)
+    hide_row(33, rows_in[1], 1)
     for c in range(0, hid.shape[3], 256):
-        hid[0, :, :, c : c + 256] = hid[0, :, :, c : c + 256] * masks[2][None]
-        hid[33, :, :, c : c + 256] = hid[33, :, :, c : c + 256] * masks[3][None]
-
-    pl.semaphore_wait(barrier, PEERS)
+        hid[0, :, :, c : c + 256] = hid[0, :, :, c : c + 256] * edge_top[None]
+        hid[33, :, :, c : c + 256] = hid[33, :, :, c : c + 256] * edge_bottom[None]
+
+    def weights(s):
+        return (
+            norm_gain[s : s + 1, :],
+            turned[s, 0],
+            qkv_w[s, :, chans : 2 * chans],
+            turned[s, 1],
+            out_w[s],
+        )
 
     def one_half(half, _):
         def mix(i, _):
-            p = lax.div(i, 8)
-            mix_row(
-                p * 2 + half, lax.rem(i, 8), p, img, depth_k, depth_b, project_w, hid, mid, moved, conv
-            )
+            p = lax.div(i, 4)
+            for k in range(2):
+                mix_row(
+                    p * 2 + half, lax.rem(i, 4) * 2 + k, p, img, depth_k, depth_b, project_w, hid,
+                    mid.at[k], moved.at[k], conv,
+                )
             return 0
 
-        lax.fori_loop(0, 16, mix, 0)
+        lax.fori_loop(0, 8, mix, 0)
 
         def attend_chunk(m, _):
             chunk = half * 4 + m
             x = jnp.concatenate([conv[w // 4, (w % 4) * 4 + m] for w in range(8)], axis=0)
-            value = window_attend(x, gain0[...], wq0[...], wk0[...], wv0[...], wo0[...])
+            value = window_attend(x, *weights(0))
             put_halves(obuf, slice(0, 512), value)
             for d in range(PEERS + 1):
                 block = [strided(obuf, 2 * d + e, 8, 64) for e in range(2)]
@@ -407,7 +473,7 @@
         blocks = recv[chunk].astype(F32)
         done = [
             set_attend(
-                blocks[:, e * 8 : e * 8 + 8].reshape(256, 256), gain1[...], wq1[...], wk1[...], wv1[...], wo1[...]
+                blocks[:, e * 8 : e * 8 + 8].reshape(256, 256), *weights(1)
             ).reshape(32, 8, 256)
             for e in range(2)
         ]
@@ -428,13 +494,18 @@
             placed[rows, pl.ds(pl.multiple_of((w % 4) * 32 + m * 8, 8), 8), :] = value
         return 0
 
-    lax.fori_loop(0, CHUNKS, finish, 0)
-
-    def store(row, _):
-        out[row] = placed[row].astype(BF16)
-        return 0
-
-    lax.fori_loop(0, 32, store, 0)
+    def finish_half(half, _):
+        lax.fori_loop(half * 4, half * 4 + 4, finish, 0)
+
+        def store(i, _):
+            row = lax.div(i, 8) * 16 + half * 8 + lax.rem(i, 8)
+            out[row] = placed[row].astype(BF16)
+            return 0
+
+        lax.fori_loop(0, 16, store, 0)
+        return 0
+
+    lax.fori_loop(0, 2, finish_half, 0)
 
     def drain(chunk, _):
         whole_wait(send, chunk, send_sem)
@@ -442,45 +513,6 @@
         return 0
 
     lax.fori_loop(0, CHUNKS, drain, 0)
-
-
-def shift_pair(first, last, axis):
-    count = lax.axis_size(axis)
-    ends = count - 1
-    before = lax.ppermute(last, axis, [(i, i + 1) for i in range(ends)])
-    after = lax.ppermute(first, axis, [(i + 1, i) for i in range(ends)])
-    return before, after
-
-
-def halo(image):
-    top, bottom = shift_pair(image[:1], image[-1:], "row")
-    img = jnp.concatenate([top, image, bottom], axis=0)
-    left, right = shift_pair(img[:, 0], img[:, -1], "col")
-    return img, left.astype(F32), right.astype(F32)
-
-
-def edge_masks():
-    row = lax.axis_index("row")
-    col = lax.axis_index("col")
-    s = jnp.arange(16)[:, None]
-    low = jnp.where((col == 0) & (s == 0), 0.0, 1.0)
-    high = jnp.where((col == lax.axis_size("col") - 1) & (s == 15), 0.0, 1.0)
-    top = jnp.where(row == 0, 0.0, 1.0) * jnp.ones((16, 1))
-    bottom = jnp.where(row == lax.axis_size("row") - 1, 0.0, 1.0) * jnp.ones((16, 1))
-    masks = jnp.stack([low, high, top, bottom]).astype(BF16)
-    return jnp.broadcast_to(masks, (4, 16, 256))
-
-
-def split_weights(norm_gain, qkv_weight, out_weight, s):
-    chans = qkv_weight.shape[1]
-    w = qkv_weight[s]
-    return (
-        norm_gain[s][None],
-        w[:, :chans].T,
-        w[:, chans : 2 * chans],
-        w[:, 2 * chans :].T,
-        out_weight[s],
-    )
 
 
 PEERS = 31
@@ -493,34 +525,34 @@
     norm_gain, qkv_weight, out_weight,
 ):
     wide = expand_weight.shape[1]
-    img, left, right = halo(image)
-    masks = edge_masks()
     blocks = pltpu.VMEM((CHUNKS, PEERS + 1, 16, 256), BF16)
     sems = pltpu.SemaphoreType.DMA((CHUNKS,))
     return pl.pallas_call(
         block_kernel,
         out_shape=jax.ShapeDtypeStruct(image.shape, BF16),
-        in_specs=[VMEM] * 21,
+        in_specs=[VMEM] * 11,
         out_specs=VMEM,
         scratch_shapes=[
-            pltpu.VMEM((2, 144, 128), F32),
+            pltpu.VMEM((2, 2, 144, 128), F32),
             pltpu.VMEM((34, 10, 16, wide), BF16),
-            pltpu.VMEM((128, wide), BF16),
-            pltpu.VMEM((2, 128, 128), F32),
+            pltpu.VMEM((2, 128, wide), BF16),
+            pltpu.VMEM((2, 2, 128, 128), F32),
             pltpu.VMEM((2, 16, 64, 256), F32),
             pltpu.VMEM((2, 512, 128), F32),
             pltpu.VMEM(image.shape, F32),
+            pltpu.VMEM((2, 128, 256), BF16),
+            pltpu.VMEM((2, 40, 256), F32),
+            pltpu.VMEM((2, 40, 256), F32),
+            pltpu.VMEM((2, 2, 256, 256), BF16),
             blocks, blocks, blocks, blocks,
-            sems, sems, sems, sems,
+            sems, sems, sems, sems, sems,
         ],
         compiler_params=pltpu.CompilerParams(
             collective_id=0, has_side_effects=True, vmem_limit_bytes=56 * 1024 * 1024
         ),
     )(
-        img, left, right, masks, bn_gain[None], bn_shift[None], expand_weight, expand_bias[None],
-        depth_kernel.reshape(9, wide), depth_bias[None], project_weight,
-        *split_weights(norm_gain, qkv_weight, out_weight, 0),
-        *split_weights(norm_gain, qkv_weight, out_weight, 1),
+        image, bn_gain[None], bn_shift[None], expand_weight, expand_bias[None],
+        depth_kernel, depth_bias[None], project_weight, norm_gain, qkv_weight, out_weight,
     )
 
 

time: 157 us -> 131 us (0.83)
  local copies, waits for them, and re-layouts: 14.9 us -> 3.13 us
  starting transfers between devices: 10.6 us -> 0 us
  other arithmetic: 4.62 us -> 0 us
  Pallas kernels: 126 us -> 128 us
    ppermute x4 -> x0, starting transfers between devices: 10.6 us -> none  [the longest x2 7.97 us: shift_pair(): before = lax.ppermute(last, axis, [(i, i + 1) for i in range(ends)])]
    unnamed x14 -> x1, local copies, waits for them, and re-layouts: 7.64 us -> 3.13 us
    concatenate x1 -> x0, other arithmetic: 3.3 us -> none  [halo(): img = jnp.concatenate([top, image, bottom], axis=0)]
    slice x5 -> x0, local copies, waits for them, and re-layouts: 2.37 us -> none  [the longest x2 1.51 us: split_weights(): w[:, chans:2 * chans]]
    concatenate x1 -> x0, local copies, waits for them, and re-layouts: 1.87 us -> none  [halo(): img = jnp.concatenate([top, image, bottom], axis=0)]
    pallas_call x1, Pallas kernels: 126 us -> 128 us  [per_device_fast(): pl.pallas_call(block_kernel, out_shape=jax.ShapeDtypeStruct(image.shape,...]
  transfers between devices with their start and end apart: 4 -> 0, of which waited for: 0 -> 0; matrix products, arithmetic and copies ran while one was open for 5% -> 0% of each run, Pallas kernels for 0% -> 0%
where the time goes in v3:
time: 131 us
  Pallas kernels  128 us (98%)
  local copies, waits for them, and re-layouts  3.13 us (2%)
    pallas_call x1, Pallas kernels, per_device_fast(): pl.pallas_call(block_kernel, out_shape=jax.ShapeDtypeStruct(image.shape,...  128 us
    unnamed x1, local copies, waits for them, and re-layouts  3.13 us

profile of v3, /device:TPU:0, one launch (start us, length us, event | category | flops | bytes accessed | tf_op | source)
XLA Modules:
  0.0 131.0 jit_solution(16328834045848023615)
XLA Ops:
  0.0 127.8 %shard_map.109 = bf16[32,128,256]{2,1,0:T(8,128)(2,1)} custom-call(bf16[32,128,256]{2,1,0:T(8,128)(2,1)} %img.1, f32[1,256]{1,0:T(1,128)} %bitcast.6, f32[1,256]{1,0:T(1,128)} %bitcast.7, bf16[256,1024]{1,0:T(8,128)(2,1)} %expand_w.1, f32[1,1024]{1,0:T(1,128)} %bitcast.4, bf16[3,3,1024]{2,1,0:T(4,128)(2,1)} %depth_k.1, f32[1,1024]{1,0:T(1,128)} %bitcast.5, ...), custom_call_target="tpu_custom_call" | custom-call | tf_op jit(solution)/shard_map/pallas_call | solution.py:530
  127.9 3.1 %copy.13 = bf16[32,128,256]{2,1,0:T(8,128)(2,1)} copy(bf16[32,128,256]{2,1,0:T(8,128)(2,1)} %shard_map.109) | data formatting | bytes 4194304

commit v4 on v3

--- a/solution.py
+++ b/solution.py
@@ -238,7 +238,7 @@
             )
             s = dot(k_p, rhs)
             s = jnp.where(low, s[:64], s[64:])
-            p = jnp.exp2(s - jnp.max(s, axis=0, keepdims=True)).astype(BF16)
+            p = jnp.exp2((s - jnp.max(s, axis=0, keepdims=True)).astype(BF16))
             p = jnp.concatenate([p * low_mask, p * high_mask], axis=0)
             lhs = jnp.concatenate([v_t[h * size : (h + 2) * size, at], ones], axis=0)
             o = dot(lhs, p)
@@ -258,7 +258,7 @@
     mixed = []
     for h in range(HEADS):
         s = dot(k, head_rows(q_t, h, size))
-        p = jnp.exp2(s - jnp.max(s, axis=0, keepdims=True)).astype(BF16)
+        p = jnp.exp2((s - jnp.max(s, axis=0, keepdims=True)).astype(BF16))
         lhs = jnp.concatenate([v_t[h * size : (h + 1) * size], ones], axis=0)
         o = dot(lhs, p)
         mixed.append((o[:size] * (1.0 / o[size : size + 1])).astype(BF16))
@@ -293,7 +293,7 @@
         hid[row, 9, :, c : c + 256] = h[9] * edge_high
 
 
-def mix_row(strip, r, slot, img, depth_k, depth_b, project_w, hid, mid, moved, conv):
+def mix_row(strip, r, slot, img, taps, depth_b, project_w, hid, mid, moved, conv):
     row = strip * WINDOW + r
     for c in range(0, hid.shape[3], 256):
         at = slice(c, c + 256)
@@ -302,7 +302,7 @@
             for u in range(3):
                 part = None
                 for v in range(3):
-                    term = hid[row + u, j0 + v : j0 + v + 4, :, at] * depth_k[u, v : v + 1, at][None]
+                    term = hid[row + u, j0 + v : j0 + v + 4, :, at] * taps[u * 3 + v, :, at][None]
                     part = term if part is None else part + term
                 part = part.astype(F32)
                 total = part if total is None else total + part
@@ -323,7 +323,7 @@
 def block_kernel(
     img, bn_gain, bn_shift, expand_w, expand_b, depth_k, depth_b, project_w,
     norm_gain, qkv_w, out_w, out,
-    rowbuf, hid, mid, moved, conv, obuf, placed, rows_in, ends_out, ends_in, turned,
+    rowbuf, hid, mid, moved, conv, obuf, placed, rows_in, ends_out, ends_in, turned, taps,
     send, recv, reply, back, halo_sem, send_sem, recv_sem, reply_sem, back_sem,
 ):
     cols = lax.axis_size("col")
@@ -390,6 +390,9 @@
         for n in range(2):
             part = qkv_w[s, :, n * 2 * chans : (n * 2 + 1) * chans]
             turned[s, n] = part.astype(F32).T.astype(BF16)
+    for n in range(9):
+        tap = depth_k[n // 3, n % 3 : n % 3 + 1, :]
+        taps[n] = jnp.broadcast_to(tap.astype(F32), taps.shape[1:]).astype(BF16)
     for row in range(32):
         cells = img[row].astype(F32)
         ends_out[0, row + 1 : row + 2, :] = cells[:1]
@@ -445,7 +448,7 @@
             p = lax.div(i, 4)
             for k in range(2):
                 mix_row(
-                    p * 2 + half, lax.rem(i, 4) * 2 + k, p, img, depth_k, depth_b, project_w, hid,
+                    p * 2 + half, lax.rem(i, 4) * 2 + k, p, img, taps, depth_b, project_w, hid,
                     mid.at[k], moved.at[k], conv,
                 )
             return 0
@@ -544,6 +547,7 @@
             pltpu.VMEM((2, 40, 256), F32),
             pltpu.VMEM((2, 40, 256), F32),
             pltpu.VMEM((2, 2, 256, 256), BF16),
+            pltpu.VMEM((9, 16, wide), BF16),
             blocks, blocks, blocks, blocks,
             sems, sems, sems, sems, sems,
         ],

time: 131 us -> 131 us (level)
  no operation moved by 1% of the time
where the time goes in v4:
time: 131 us; the launch traced here: 130 us
  Pallas kernels  127 us (97%)
  local copies, waits for them, and re-layouts  3.13 us (2%)
    pallas_call x1, Pallas kernels, per_device_fast(): pl.pallas_call(block_kernel, out_shape=jax.ShapeDtypeStruct(image.shape,...  127 us
    unnamed x1, local copies, waits for them, and re-layouts  3.13 us

profile of v4, /device:TPU:0, one launch (start us, length us, event | category | flops | bytes accessed | tf_op | source)
XLA Modules:
  0.0 130.4 jit_solution(8079858702438524061)
XLA Ops:
  0.0 127.3 %shard_map.109 = bf16[32,128,256]{2,1,0:T(8,128)(2,1)} custom-call(bf16[32,128,256]{2,1,0:T(8,128)(2,1)} %img.1, f32[1,256]{1,0:T(1,128)} %bitcast.6, f32[1,256]{1,0:T(1,128)} %bitcast.7, bf16[256,1024]{1,0:T(8,128)(2,1)} %expand_w.1, f32[1,1024]{1,0:T(1,128)} %bitcast.4, bf16[3,3,1024]{2,1,0:T(4,128)(2,1)} %depth_k.1, f32[1,1024]{1,0:T(1,128)} %bitcast.5, ...), custom_call_target="tpu_custom_call" | custom-call | tf_op jit(solution)/shard_map/pallas_call | solution.py:533
  127.3 3.1 %copy.13 = bf16[32,128,256]{2,1,0:T(8,128)(2,1)} copy(bf16[32,128,256]{2,1,0:T(8,128)(2,1)} %shard_map.109) | data formatting | bytes 4194304
